TPU v7x, 32 devices: a whole 2x2x4 slice. The times are simulated.
32 devices in a mesh: fsdp: 8 (over z, y), dp: 4 (over x, core).
Axes of the slice: x: 2, y: 2, z: 4, core: 2. Of those that a mesh axis runs over, the one named last changes fastest.
Arguments:
- images: bfloat16 [64, 14, 14, 2048], P(('fsdp', 'dp')), may hold values from -24 to 24
- valid: int32 [64], P(('fsdp', 'dp')), may hold values from 0 to 1, as said below
- cotangent: bfloat16 [64, 14, 14, 2048], P(('fsdp', 'dp')), may hold values from -24 to 24
- w_reduce: bfloat16 [2048, 1024], P('fsdp'), may hold values from -0.125 to 0.125
- gain_one: bfloat16 [1024], P('fsdp'), may hold values from 0.25 to 1.75
- shift_one: bfloat16 [1024], P('fsdp'), may hold values from -3 to 3
- w_group: bfloat16 [288, 1024], P('fsdp'), may hold values from -0.375 to 0.375
- gain_two: bfloat16 [1024], P('fsdp'), may hold values from 0.25 to 1.75
- shift_two: bfloat16 [1024], P('fsdp'), may hold values from -3 to 3
- w_expand: bfloat16 [1024, 2048], P('fsdp'), may hold values from -0.1875 to 0.1875
- gain_three: bfloat16 [2048], P('fsdp'), may hold values from 0.25 to 1.75
- shift_three: bfloat16 [2048], P('fsdp'), may hold values from -3 to 3
Outputs:
- output: bfloat16 [64, 14, 14, 2048], P(('fsdp', 'dp'))
- grad_input: bfloat16 [64, 14, 14, 2048], P(('fsdp', 'dp'))
- grad_w_reduce: float32 [2048, 1024], P('fsdp')
- grad_w_group: float32 [288, 1024], P('fsdp')
- grad_w_expand: float32 [1024, 2048], P('fsdp')
- grad_gain_one: float32 [1024], P('fsdp')
- grad_shift_one: float32 [1024], P('fsdp')
- grad_gain_two: float32 [1024], P('fsdp')
- grad_shift_two: float32 [1024], P('fsdp')
- grad_gain_three: float32 [2048], P('fsdp')
- grad_shift_three: float32 [2048], P('fsdp')
Inputs may be any that keep to these rules, and one draw needn't show every extreme that they name: At least one slot of all is valid; each slot is valid with probability 9/10.
All inputs are finite; a program needn't handle non-finite values.
Results may differ from a plain program's by a relative error of at most 0.0075.
Values may be sent and summed in bfloat16 or wider, within the bound.
No kernel may reach another device: no remote copies, remote signals or barrier semaphores. Data moves between devices by JAX's collectives and lax.ppermute only.
A program may use at most 192 MiB of HBM per device.

v0:
```python
import jax
import jax.numpy as jnp
from jax import lax
from jax.sharding import PartitionSpec as P

GROUPS = 32


epsilon = 1e-05


def dsilu(values):
    sigma = jax.nn.sigmoid(values)
    return sigma * (1.0 + values * (1.0 - sigma))


def fetch_forward(weight, gain, shift):
    return (
        lax.all_gather(weight, "fsdp", axis=0, tiled=True),
        lax.all_gather(gain, "fsdp", axis=0, tiled=True),
        lax.all_gather(shift, "fsdp", axis=0, tiled=True),
    )


def fetch_backward(weight, gain, shift):
    return (
        lax.all_gather(weight, "fsdp", axis=0, tiled=True),
        lax.all_gather(gain, "fsdp", axis=0, tiled=True),
        lax.all_gather(shift, "fsdp", axis=0, tiled=True),
    )


def global_moments(hidden, pixel_mask, valid):
    first = jnp.sum(pixel_mask * hidden, axis=(0, 1, 2))
    second = jnp.sum(pixel_mask * hidden * hidden, axis=(0, 1, 2))
    pixels = jnp.sum(valid.astype(jnp.float32)) * (hidden.shape[1] * hidden.shape[2])
    return lax.psum((first, second, pixels), ("fsdp", "dp"))


def normalize(hidden, moments, gain, shift):
    first, second, pixels = moments
    mean = first / pixels
    inverse = lax.rsqrt(second / pixels - mean * mean + epsilon)
    normed = (hidden - mean) * inverse
    return (normed * gain.astype(jnp.float32) + shift.astype(jnp.float32), normed, inverse)


def norm_backward(grad_out, normed, inverse, gain, pixels, pixel_mask):
    masked = pixel_mask * grad_out
    total_shift, total_gain = lax.psum(
        (jnp.sum(masked, axis=(0, 1, 2)), jnp.sum(masked * normed, axis=(0, 1, 2))), ("fsdp", "dp")
    )
    grad_hidden = (
        gain.astype(jnp.float32)
        * inverse
        * (grad_out - pixel_mask * (total_shift + normed * total_gain) / pixels)
    )
    return (grad_hidden.astype(jnp.bfloat16), total_gain, total_shift)


def row_shards(function, rows):
    return lax.psum_scatter(
        function(jnp.int32(0), lax.axis_size("fsdp") * rows),
        "fsdp",
        scatter_dimension=0,
        tiled=True,
    )


def gather_patches(activation):
    side = activation.shape[1]
    padded = jnp.pad(activation, ((0, 0), (1, 1), (1, 1), (0, 0)))
    return jnp.stack(
        [
            padded[:, vertical : vertical + side, lateral : lateral + side]
            for vertical in range(3)
            for lateral in range(3)
        ],
        axis=3,
    )


def per_device(
    images,
    valid,
    cotangent,
    w_reduce,
    gain_one,
    shift_one,
    w_group,
    gain_two,
    shift_two,
    w_expand,
    gain_three,
    shift_three,
):
    image_count = images.shape[0]
    side = images.shape[1]
    channels = images.shape[3]
    width = w_reduce.shape[1]
    group_width = width // GROUPS
    pixel_mask = valid.astype(jnp.float32).reshape(image_count, 1, 1, 1)
    flat_input = images.reshape(-1, channels)
    weight_one, gain_a, shift_a = fetch_forward(w_reduce, gain_one, shift_one)
    reduced = jnp.dot(flat_input, weight_one, preferred_element_type=jnp.float32).reshape(
        image_count, side, side, width
    )
    moments_one = global_moments(reduced, pixel_mask, valid)
    normal_one, normed_one, inverse_one = normalize(reduced, moments_one, gain_a, shift_a)
    act_one = jax.nn.silu(normal_one).astype(jnp.bfloat16)
    weight_two, gain_b, shift_b = fetch_forward(w_group, gain_two, shift_two)
    kernel = weight_two.reshape(9, group_width, GROUPS, group_width)
    patches = gather_patches(act_one).reshape(image_count, side, side, 9, GROUPS, group_width)
    grouped = jnp.einsum(
        "nhwtgi,tigo->nhwgo", patches, kernel, preferred_element_type=jnp.float32
    ).reshape(image_count, side, side, width)
    moments_two = global_moments(grouped, pixel_mask, valid)
    normal_two, normed_two, inverse_two = normalize(grouped, moments_two, gain_b, shift_b)
    act_two = jax.nn.silu(normal_two).astype(jnp.bfloat16)
    weight_three, gain_c, shift_c = fetch_forward(w_expand, gain_three, shift_three)
    flat_two = act_two.reshape(-1, width)
    expanded = jnp.dot(flat_two, weight_three, preferred_element_type=jnp.float32).reshape(
        image_count, side, side, channels
    )
    moments_three = global_moments(expanded, pixel_mask, valid)
    normal_three, normed_three, inverse_three = normalize(expanded, moments_three, gain_c, shift_c)
    summed = normal_three + images.astype(jnp.float32)
    output = (jax.nn.silu(summed) * pixel_mask).astype(jnp.bfloat16)
    weight_one, gain_a, shift_a = fetch_backward(w_reduce, gain_one, shift_one)
    weight_two, gain_b, shift_b = fetch_backward(w_group, gain_two, shift_two)
    weight_three, gain_c, shift_c = fetch_backward(w_expand, gain_three, shift_three)
    kernel = weight_two.reshape(9, group_width, GROUPS, group_width)
    pixels = moments_one[2]
    grad_summed = cotangent.astype(jnp.float32) * pixel_mask * dsilu(summed)
    grad_expanded, gain_total_three, shift_total_three = norm_backward(
        grad_summed, normed_three, inverse_three, gain_c, pixels, pixel_mask
    )
    flat_grad_three = grad_expanded.reshape(-1, channels)

    def expand_rows(start, count):
        return lax.dot_general(
            flat_two, flat_grad_three, (((0,), (0,)), ((), ())), preferred_element_type=jnp.float32
        )

    part_expand = row_shards(expand_rows, w_expand.shape[0])
    grad_act_two = lax.dot_general(
        flat_grad_three, weight_three, (((1,), (1,)), ((), ())), preferred_element_type=jnp.float32
    )
    grad_act_two = grad_act_two.reshape(image_count, side, side, width)
    grad_grouped, gain_total_two, shift_total_two = norm_backward(
        grad_act_two * dsilu(normal_two), normed_two, inverse_two, gain_b, pixels, pixel_mask
    )
    grouped_grad = grad_grouped.reshape(image_count, side, side, GROUPS, group_width)
    kernel_term = jnp.einsum(
        "nhwtgi,nhwgo->tigo", patches, grouped_grad, preferred_element_type=jnp.float32
    ).reshape(9 * group_width, width)

    def group_rows(start, count):
        return kernel_term

    part_group = row_shards(group_rows, w_group.shape[0])
    grad_padded = jnp.zeros((image_count, side + 2, side + 2, width), jnp.float32)
    for tap_index in range(9):
        vertical, lateral = divmod(tap_index, 3)
        contribution = jnp.einsum(
            "nhwgo,igo->nhwgi", grouped_grad, kernel[tap_index], preferred_element_type=jnp.float32
        )
        grad_padded = grad_padded.at[:, vertical : vertical + side, lateral : lateral + side].add(
            contribution.reshape(image_count, side, side, width)
        )
    grad_act_one = grad_padded[:, 1 : side + 1, 1 : side + 1]
    grad_reduced, gain_total_one, shift_total_one = norm_backward(
        grad_act_one * dsilu(normal_one), normed_one, inverse_one, gain_a, pixels, pixel_mask
    )
    flat_grad_one = grad_reduced.reshape(-1, width)

    def reduce_rows(start, count):
        return lax.dot_general(
            flat_input, flat_grad_one, (((0,), (0,)), ((), ())), preferred_element_type=jnp.float32
        )

    part_reduce = row_shards(reduce_rows, w_reduce.shape[0])
    back_input = lax.dot_general(
        flat_grad_one, weight_one, (((1,), (1,)), ((), ())), preferred_element_type=jnp.float32
    )
    grad_input = (back_input.reshape(images.shape) + grad_summed).astype(jnp.bfloat16)
    grad_w_reduce, grad_w_group, grad_w_expand = lax.psum(
        (part_reduce, part_group, part_expand), "dp"
    )
    position = lax.axis_index("fsdp")

    def own_shard(total, shard):
        return lax.dynamic_slice_in_dim(total, position * shard, shard, 0)

    inner = gain_one.shape[0]
    outer = gain_three.shape[0]
    return (
        output,
        grad_input,
        grad_w_reduce,
        grad_w_group,
        grad_w_expand,
        own_shard(gain_total_one, inner),
        own_shard(shift_total_one, inner),
        own_shard(gain_total_two, inner),
        own_shard(shift_total_two, inner),
        own_shard(gain_total_three, outer),
        own_shard(shift_total_three, outer),
    )


def solution(mesh):
    return jax.shard_map(
        per_device,
        mesh=mesh,
        in_specs=(
            P(("fsdp", "dp"), None, None, None),
            P(("fsdp", "dp")),
            P(("fsdp", "dp"), None, None, None),
            P("fsdp", None),
            P("fsdp"),
            P("fsdp"),
            P("fsdp", None),
            P("fsdp"),
            P("fsdp"),
            P("fsdp", None),
            P("fsdp"),
            P("fsdp"),
        ),
        out_specs=(
            P(("fsdp", "dp"), None, None, None),
            P(("fsdp", "dp"), None, None, None),
            P("fsdp", None),
            P("fsdp", None),
            P("fsdp", None),
            P("fsdp"),
            P("fsdp"),
            P("fsdp"),
            P("fsdp"),
            P("fsdp"),
            P("fsdp"),
        ),
        check_vma=False,
    )
```

profile of v0, /device:TPU:0, one launch (start us, length us, event | category | flops | bytes accessed | tf_op | source)
XLA Modules:
  0.0 1079.0 jit_solution(13013466040822468438)
XLA Ops:
  10.7 22.4 %all-gather = bf16[8,1,128]{2,1,0:T(2,128)(2,1)S(1)} all-gather(bf16[1,1,128]{2,1,0:T(2,128)(2,1)} %bitcast.148), channel_id=1, replica_groups=mesh['fsdp'=8,'dp'=4] {'fsdp'}, dimensions={0}, use_global_device_ids=true | all-gather | bytes 2304 | tf_op jit(solution)/shard_map/all_gather | solution.py:20
  33.1 16.5 %all-gather.1 = bf16[8,1,128]{2,1,0:T(2,128)(2,1)S(1)} all-gather(bf16[1,1,128]{2,1,0:T(2,128)(2,1)} %bitcast.149), channel_id=1, replica_groups=mesh['fsdp'=8,'dp'=4] {'fsdp'}, dimensions={0}, use_global_device_ids=true | all-gather | bytes 2304 | tf_op jit(solution)/shard_map/all_gather | solution.py:21
  49.6 33.7 %all-gather.2 = bf16[8,36,1024]{2,1,0:T(8,128)(2,1)S(1)} all-gather(bf16[1,36,1024]{2,1,0:T(8,128)(2,1)} %bitcast.132), channel_id=1, replica_groups=mesh['fsdp'=8,'dp'=4] {'fsdp'}, dimensions={0}, use_global_device_ids=true | all-gather | bytes 663552 | tf_op jit(solution)/shard_map/all_gather | solution.py:19
  86.2 18.1 %all-gather.3 = bf16[8,1,128]{2,1,0:T(2,128)(2,1)S(1)} all-gather(bf16[1,1,128]{2,1,0:T(2,128)(2,1)S(1)} %bitcast.150), channel_id=1, replica_groups=mesh['fsdp'=8,'dp'=4] {'fsdp'}, dimensions={0}, use_global_device_ids=true | all-gather | bytes 2304 | tf_op jit(solution)/shard_map/all_gather | solution.py:20
  104.3 16.3 %all-gather.4 = bf16[8,1,128]{2,1,0:T(2,128)(2,1)S(1)} all-gather(bf16[1,1,128]{2,1,0:T(2,128)(2,1)S(1)} %bitcast.151), channel_id=1, replica_groups=mesh['fsdp'=8,'dp'=4] {'fsdp'}, dimensions={0}, use_global_device_ids=true | all-gather | bytes 2304 | tf_op jit(solution)/shard_map/all_gather | solution.py:21
  120.7 18.5 %all-gather.5 = bf16[8,1,256]{2,1,0:T(2,128)(2,1)S(1)} all-gather(bf16[1,1,256]{2,1,0:T(2,128)(2,1)S(1)} %reshape.546), channel_id=1, replica_groups=mesh['fsdp'=8,'dp'=4] {'fsdp'}, dimensions={0}, use_global_device_ids=true | all-gather | bytes 4608 | tf_op jit(solution)/shard_map/all_gather | solution.py:20
  139.2 16.6 %all-gather.6 = bf16[8,1,256]{2,1,0:T(2,128)(2,1)S(1)} all-gather(bf16[1,1,256]{2,1,0:T(2,128)(2,1)S(1)} %reshape.548), channel_id=1, replica_groups=mesh['fsdp'=8,'dp'=4] {'fsdp'}, dimensions={0}, use_global_device_ids=true | all-gather | bytes 4608 | tf_op jit(solution)/shard_map/all_gather | solution.py:21
  156.5 4.8 fusion.31
  161.3 37.9 %all-reduce.9 = (f32[1024]{0:T(1024)S(1)}, f32[]{:T(128)}, f32[1024]{0:T(1024)S(1)}) all-reduce(f32[1024]{0:T(1024)S(1)} %get-tuple-element.163, f32[]{:T(128)S(6)} %mul.280, f32[1024]{0:T(1024)S(1)} %get-tuple-element.162), channel_id=1, replica_groups=mesh['fsdp'=8,'dp'=4] {'fsdp','dp'}, use_global_device_ids=true, to_apply=%region_1.0 | all-reduce | flops 2049 | bytes 16392 | tf_op jit(solution)/shard_map/psum | solution.py:37
  208.9 4.9 reshape.574
  235.7 5.3 reshape.582
  241.0 5.3 copy_dynamic-update-slice_fusion.8
  272.7 17.0 %multiply_reduce_fusion = (f32[32,32]{1,0:T(8,128)S(1)}, f32[32,32]{1,0:T(8,128)S(1)}, f32[2,14,14,32,32]{4,2,1,0,3:T(8,128)}) fusion(f32[2]{0:T(128)S(1)} %convert_element_type.58, bf16[2,14,14,9,32,32]{5,2,3,1,0,4:T(8,128)(2,1)} %copy_dynamic-update-slice_fusion, bf16[9,32,32,32,1,1]{3,2,1,0,5,4:T(8,128)(2,1)S(1)} %bitcast.122), kind=kOutput, calls=%fused_computation.3 | convolution fusion | flops 232814592 | bytes 9429000 | tf_op jit(solution)/shard_map/nhwtgi,tigo->nhwgo/dot_general | solution.py:114
  289.9 9.5 copy.233
  299.4 5.1 reshape.583
  304.5 42.4 %all-reduce.8 = (f32[1024]{0:T(1024)S(1)}, f32[1024]{0:T(1024)S(1)}) all-reduce(f32[1024]{0:T(1024)S(1)} %reduce_sum.135, f32[1024]{0:T(1024)S(1)} %reduce_sum.133), channel_id=1, replica_groups=mesh['fsdp'=8,'dp'=4] {'fsdp','dp'}, use_global_device_ids=true, to_apply=%region_9.10 | all-reduce | flops 2048 | bytes 16384 | tf_op jit(solution)/shard_map/psum | solution.py:37
  347.6 6.6 fusion.12
  354.2 39.0 %all-reduce.7 = (f32[2048]{0:T(1024)S(1)}, f32[2048]{0:T(1024)S(1)}) all-reduce(f32[2048]{0:T(1024)S(1)} %get-tuple-element.157, f32[2048]{0:T(1024)S(1)} %get-tuple-element.156), channel_id=1, replica_groups=mesh['fsdp'=8,'dp'=4] {'fsdp','dp'}, use_global_device_ids=true, to_apply=%region_11.12 | all-reduce | flops 4096 | bytes 32768 | tf_op jit(solution)/shard_map/psum | solution.py:37
  394.5 6.5 multiply_reduce_fusion.3
  401.0 41.4 %all-reduce.6 = (f32[2048]{0:T(1024)S(1)}, f32[2048]{0:T(1024)S(1)}) all-reduce(f32[2048]{0:T(1024)S(1)} %get-tuple-element.155, f32[2048]{0:T(1024)S(1)} %get-tuple-element.154), channel_id=1, replica_groups=mesh['fsdp'=8,'dp'=4] {'fsdp','dp'}, use_global_device_ids=true, to_apply=%region_17.18 | all-reduce | flops 4096 | bytes 32768 | tf_op jit(solution)/shard_map/psum | solution.py:50
  442.4 4.9 multiply_convert_fusion
  448.5 5.8 convolution_bitcast_fusion
  464.8 6.9 multiply_reduce_fusion.8
  471.7 41.1 %all-reduce.5 = (f32[1024]{0:T(1024)S(1)}, f32[1024]{0:T(1024)S(1)}) all-reduce(f32[1024]{0:T(1024)S(1)} %get-tuple-element.161, f32[1024]{0:T(1024)S(1)} %get-tuple-element.160), channel_id=1, replica_groups=mesh['fsdp'=8,'dp'=4] {'fsdp','dp'}, use_global_device_ids=true, to_apply=%region_21.22 | all-reduce | flops 2048 | bytes 16384 | tf_op jit(solution)/shard_map/psum | solution.py:50
  517.3 4.1 reshape.522
  521.4 4.1 convolution_bitcast_fusion.9
  525.5 6.5 copy.239
  532.0 6.1 reshape.585
  542.2 6.5 copy.236
  548.7 6.2 reshape.584
  554.9 4.1 convolution_bitcast_fusion.8
  559.0 6.5 copy.242
  565.4 6.2 reshape.586
  577.9 11.6 %scatter-add.31 = f32[2,16,16,1024]{3,2,1,0:T(8,128)} dynamic-update-slice(f32[2,16,16,1024]{3,2,1,0:T(8,128)} %scatter-add.30, f32[2,14,14,1024]{3,2,1,0:T(8,128)} %dynamic-slice_add_fusion, s32[]{:T(128)} %constant.287.clone.1, s32[]{:T(128)} %bitcast.23, s32[]{:T(128)} %bitcast.24, s32[]{:T(128)} %constant.287.clone.1) | dynamic-update-slice | bytes 3211268 | tf_op jit(solution)/shard_map/scatter-add | solution.py:168
  589.5 5.8 add_select_fusion
  595.3 11.9 %scatter-add.34 = f32[2,16,16,1024]{3,2,1,0:T(8,128)} dynamic-update-slice(f32[2,16,16,1024]{3,2,1,0:T(8,128)} %scatter-add.31, f32[2,14,14,1024]{3,2,1,0:T(8,128)} %add_select_fusion, s32[]{:T(128)} %constant.287.clone.1, s32[]{:T(128)} %bitcast.27, s32[]{:T(128)} %bitcast.28, s32[]{:T(128)} %constant.287.clone.1) | dynamic-update-slice | bytes 3211268 | tf_op jit(solution)/shard_map/scatter-add | solution.py:168
  611.4 6.5 copy.245
  617.8 6.1 reshape.587
  628.1 6.5 copy.248
  634.6 6.0 reshape.588
  644.3 10.2 scatter-add.35
  658.3 10.4 scatter-add.36
  672.8 6.5 copy.251
  679.3 6.4 reshape.589
  689.8 6.5 copy.254
  696.2 6.0 reshape.590
  706.0 10.2 scatter-add.39
  720.0 10.2 scatter-add.40
  734.3 6.5 copy.257
  740.8 6.0 reshape.591
  750.6 10.3 scatter-add.41
  764.0 6.5 copy.260
  770.5 6.0 reshape.592
  780.3 10.1 scatter-add.44
  790.5 4.5 multiply_reduce_fusion.7
  795.0 41.4 %all-reduce.4 = (f32[1024]{0:T(1024)S(1)}, f32[1024]{0:T(1024)S(1)}) all-reduce(f32[1024]{0:T(1024)S(1)} %get-tuple-element.159, f32[1024]{0:T(1024)S(1)} %get-tuple-element.158), channel_id=1, replica_groups=mesh['fsdp'=8,'dp'=4] {'fsdp','dp'}, use_global_device_ids=true, to_apply=%region_26.27 | all-reduce | flops 2048 | bytes 16384 | tf_op jit(solution)/shard_map/psum | solution.py:50
  840.7 5.9 convolution_bitcast_fusion.1
  846.7 17.4 %fusion.17 = f32[9,32,32,32]{1,3,0,2:T(8,128)} fusion(bf16[2,14,14,9,32,32]{5,2,3,1,0,4:T(8,128)(2,1)} %copy_dynamic-update-slice_fusion, bf16[2,14,14,32,32,1]{4,3,0,2,1,5:T(8,128)(2,1)S(1)} %bitcast.121), kind=kOutput, calls=%fused_computation.51 | convolution fusion | flops 231211008 | bytes 9207808 | tf_op jit(solution)/shard_map/nhwtgi,nhwgo->tigo/dot_general | solution.py:154
  864.1 6.8 copy.192
  870.8 4.2 reshape.535
  875.0 43.4 %fusion = f32[40,1024]{1,0:T(8,128)S(1)} fusion(f32[288,1024]{1,0:T(8,128)S(1)} %reshape.535), kind=kCustom, calls=%all-reduce-scatter | all-reduce-scatter fusion | flops 327681 | bytes 1344000
  924.2 87.1 %reduce-scatter.5.cloned.1.call-done = f32[256,1024]{0,1:T(8,128)} async-done(((f32[2048,1024]{0,1:T(8,128)}), f32[256,1024]{0,1:T(8,128)}) %reduce-scatter.5.cloned.1.call-update) | async-done | bytes 1048592 | tf_op jit(solution)/shard_map/reduce_scatter | solution.py:62
  1017.6 5.8 add_convert_fusion
  1029.1 38.6 %all-reduce.13.cloned.1.call-done = (f32[256,1024]{0,1:T(8,128)}, f32[36,1024]{1,0:T(8,128)}, f32[128,2048]{1,0:T(8,128)}) async-done(((f32[256,1024]{0,1:T(8,128)}, f32[36,1024]{1,0:T(8,128)}, f32[128,2048]{1,0:T(8,128)}), (f32[256,1024]{0,1:T(8,128)}, f32[36,1024]{1,0:T(8,128)}, f32[128,2048]{1,0:T(8,128)})) %all-reduce.13.cloned.1.call-update) | async-done | bytes 2244624 | tf_op jit(solution)/shard_map/psum | solution.py:187
  (191 shorter events, 164.9 us)
Async XLA Ops:
  7.2 149.3 %all-gather.10.cloned.1.call-start = ((), (), s32[]{:S(2)}) async-start(), calls=%async_computation.2 | async-start | bytes 4718592 | tf_op jit(solution)/shard_map/all_gather | solution.py:19
  7.9 78.3 %copy-start.40 = (bf16[128]{0:T(256)(128)(2,1)S(1)}, bf16[128]{0:T(256)(128)(2,1)}, u32[]{:S(2)}) copy-start(bf16[128]{0:T(256)(128)(2,1)} %param.37) | copy-start | bytes 772
  7.9 96.4 %copy-start.41 = (bf16[128]{0:T(256)(128)(2,1)S(1)}, bf16[128]{0:T(256)(128)(2,1)}, u32[]{:S(2)}) copy-start(bf16[128]{0:T(256)(128)(2,1)} %param.38) | copy-start | bytes 772
  7.9 112.7 %copy-start.44 = (bf16[256]{0:T(256)(128)(2,1)S(1)}, bf16[256]{0:T(256)(128)(2,1)}, u32[]{:S(2)}) copy-start(bf16[256]{0:T(256)(128)(2,1)} %param.40) | copy-start | bytes 1540
  7.9 131.3 %copy-start.45 = (bf16[256]{0:T(256)(128)(2,1)S(1)}, bf16[256]{0:T(256)(128)(2,1)}, u32[]{:S(2)}) copy-start(bf16[256]{0:T(256)(128)(2,1)} %param.41) | copy-start | bytes 1540
  8.0 148.6 %copy-start.21 = (bf16[2,14,14,2048]{3,0,2,1:T(2,128)(2,1)S(1)}, bf16[2,14,14,2048]{3,0,2,1:T(2,128)(2,1)}, u32[]{:S(2)}) copy-start(bf16[2,14,14,2048]{3,0,2,1:T(2,128)(2,1)} %param.30) | copy-start | bytes 4816900
  8.0 339.6 %all-gather.12.cloned.1.call-start = ((), (), s32[]{:S(2)}) async-start(), calls=%async_computation.3 | async-start | bytes 4718592 | tf_op jit(solution)/shard_map/all_gather | solution.py:19
  8.7 915.4 %reduce-scatter.7.cloned.1.call-start = ((), (), s32[]{:S(2)}) async-start(), calls=%async_computation.5 | async-start | bytes 9437184 | tf_op jit(solution)/shard_map/reduce_scatter | solution.py:62
  33.1 168.0 %copy-start.29 = (f32[8,1,128]{2,1,0:T(1,128)}, f32[8,1,128]{2,1,0:T(1,128)S(1)}, u32[]{:S(2)}) copy-start(f32[8,1,128]{2,1,0:T(1,128)S(1)} %convert_element_type.74) | copy-start | bytes 12292
  49.6 151.5 %copy-start.33 = (f32[8,1,128]{2,1,0:T(1,128)}, f32[8,1,128]{2,1,0:T(1,128)S(1)}, u32[]{:S(2)}) copy-start(f32[8,1,128]{2,1,0:T(1,128)S(1)} %convert_element_type.75) | copy-start | bytes 12292
  83.4 73.1 %copy-start.11 = (bf16[8,36,1024]{2,1,0:T(8,128)(2,1)}, bf16[8,36,1024]{2,1,0:T(8,128)(2,1)S(1)}, u32[]{:S(2)}) copy-start(bf16[8,36,1024]{2,1,0:T(8,128)(2,1)S(1)} %all-gather.2) | copy-start | bytes 1769476
  161.3 44.1 %copy-start = (f32[2,14,14,1024]{3,2,1,0:T(8,128)}, f32[2,14,14,1024]{3,2,1,0:T(8,128)S(1)}, u32[]{:S(2)}) copy-start(f32[2,14,14,1024]{3,2,1,0:T(8,128)S(1)} %get-tuple-element.211) | copy-start | bytes 4816900
  200.4 0.7 copy-start.27
  201.1 4.3 copy-start.31
  208.9 4.9 copy-start.17
  213.8 3.6 copy-start.16
  217.4 3.6 copy-start.15
  221.0 3.6 copy-start.14
  224.6 3.7 copy-start.13
  241.0 5.3 copy-start.8
  246.3 3.2 copy-start.7
  249.5 3.3 copy-start.6
  252.8 3.3 copy-start.2
  256.1 3.3 copy-start.5
  259.4 3.3 copy-start.4
  266.0 3.2 copy-start.3
  269.3 3.5 copy-start.18
  347.6 46.9 %copy-start.20 = (bf16[2,14,14,2048]{3,0,2,1:T(2,128)(2,1)S(1)}, bf16[2,14,14,2048]{3,0,2,1:T(2,128)(2,1)}, u32[]{:S(2)}) copy-start(bf16[2,14,14,2048]{3,0,2,1:T(2,128)(2,1)} %param.32) | copy-start | bytes 4816900
  442.4 4.9 copy-start.36
  442.4 4.9 copy-start.37
  447.3 1.2 copy-start.19
  454.3 1.1 copy-start.12
  454.3 556.9 %reduce-scatter.5.cloned.1.call-start = ((), (), s32[]{:S(2)}) async-start(), calls=%async_computation.4 | async-start | bytes 9437184 | tf_op jit(solution)/shard_map/reduce_scatter | solution.py:62
  455.5 8.6 copy-start.43
  512.8 2.7 copy-start.38
  512.8 2.7 copy-start.39
  571.6 3.3 copy-start.1
  571.6 3.3 copy-start.10
  780.3 10.1 copy-start.28
  780.3 10.1 copy-start.30
  780.3 10.1 copy-start.32
  780.3 10.1 copy-start.34
  790.5 45.9 %copy-start.35 = (f32[1024]{0:T(1024)S(1)}, f32[1024]{0:T(1024)}, u32[]{:S(2)}) copy-start(f32[1024]{0:T(1024)} %get-tuple-element.180) | copy-start | bytes 12292
  836.4 4.3 copy-start.22
  839.7 0.9 copy-start.24
  846.6 221.1 %all-reduce.13.cloned.1.call-start = ((), (), s32[]{:S(2)}) async-start(), calls=%async_computation.6 | async-start | bytes 4521984 | tf_op jit(solution)/shard_map/psum | solution.py:187
  870.8 49.7 %copy-start.42 = (u32[32]{0:T(128)S(1)}, u32[32]{0:T(128)}, u32[]{:S(2)}) copy-start(u32[32]{0:T(128)} %constant.309) | copy-start | bytes 388
  875.0 142.6 %copy-start.25 = (bf16[2,14,14,1024]{3,2,1,0:T(8,128)(2,1)S(1)}, bf16[2,14,14,1024]{3,2,1,0:T(8,128)(2,1)}, u32[]{:S(2)}) copy-start(bf16[2,14,14,1024]{3,2,1,0:T(8,128)(2,1)} %copy-done.24) | copy-start | bytes 2408452
  918.4 4.6 collective-permute-start
  1023.4 2.8 copy-start.9
  1067.7 2.6 copy-start.26
  1067.7 3.3 copy-start.23
Sparse Core Ops, SparseCore 0:
  10.1 86.3 all-gather.9
  98.7 72.7 all-gather.11
  454.5 149.3 reduce-scatter.6
  846.7 164.4 reduce-scatter.4
  1014.2 53.3 all-reduce.12
where the time goes:
time: 1090 us; the launch traced here: 1080 us
  blocking collectives  429 us (39%)
  local copies, waits for them, and re-layouts  337 us (31%)
  waiting for transfers between devices  128 us (12%)
  matrix products  106 us (10%)
  other arithmetic  60.5 us (6%)
  between operations  16.2 us (1%)
    psum x3, blocking collectives, norm_backward(): lax.psum((jnp.sum(masked, axis=(0, 1, 2)), jnp.sum(masked * normed, axis=...  124 us
    psum x3, blocking collectives, global_moments(): return lax.psum((first, second, pixels), ('fsdp', 'dp'))  119 us
    another operation x19, local copies, waits for them, and re-layouts  102 us
    scatter-add x9, local copies, waits for them, and re-layouts, per_device(): grad_padded.at[:, vertical:vertical + side, lateral:lateral + side]  88.3 us
    reduce_scatter x2, waiting for transfers between devices, row_shards(): lax.psum_scatter(function(jnp.int32(0), lax.axis_size('fsdp') * rows), 'f...  87.1 us
    all_gather x3, blocking collectives, fetch_forward(): lax.all_gather(gain, 'fsdp', axis=0, tiled=True)  59.1 us
    all_gather x3, blocking collectives, fetch_forward(): lax.all_gather(shift, 'fsdp', axis=0, tiled=True)  49.5 us
    unnamed x1, blocking collectives  43.4 us
  transfers between devices with their start and end apart: 6, of which 3 were waited for; matrix products, arithmetic and copies ran while one was open for 48% of the time, Pallas kernels for 0%

commit v1 on v0

v1 whole, which is shorter than its diff:
```python
import functools

import jax
import jax.numpy as jnp
from jax import lax
from jax.experimental import pallas as pl
from jax.experimental.pallas import tpu as pltpu
from jax.sharding import Mesh
from jax.sharding import PartitionSpec as P

GROUPS = 32
TAPS = 9
LINE = 16
BLOCK = 256
epsilon = 1e-05
BF16, F32 = jnp.bfloat16, jnp.float32
SWAP = [(0, 1), (1, 0)]


def sigmoid(values):
    return 0.5 * jnp.tanh(0.5 * values) + 0.5


def dsilu(values):
    sigma = sigmoid(values)
    return sigma * (1.0 + values * (1.0 - sigma))


def dot(a, b, contract=((1,), (0,))):
    return lax.dot_general(a, b, (contract, ((), ())), preferred_element_type=F32)


NT = ((1,), (1,))
TN = ((0,), (0,))


def call(kernel, outs, *args, scalars=0, scratch=(), vmem=40, name=None, flops=0):
    vm = pl.BlockSpec(memory_space=pltpu.VMEM)
    sm = pl.BlockSpec(memory_space=pltpu.SMEM)
    many = isinstance(outs, (list, tuple))
    return pl.pallas_call(
        kernel,
        out_shape=outs,
        in_specs=[sm] * scalars + [vm] * (len(args) - scalars),
        out_specs=[vm] * len(outs) if many else vm,
        scratch_shapes=list(scratch),
        compiler_params=pltpu.CompilerParams(vmem_limit_bytes=vmem << 20),
        cost_estimate=pl.CostEstimate(flops=flops, bytes_accessed=1 << 20, transcendentals=0),
        name=name,
    )(*args)


def shape(dims, dtype):
    return jax.ShapeDtypeStruct(dims, dtype)


def moments(total, pixels):
    mean = total[0:1, :] / pixels
    inverse = lax.rsqrt(total[1:2, :] / pixels - mean * mean + epsilon)
    return mean, inverse


def line_mask(columns):
    return lax.broadcasted_iota(jnp.int32, (LINE, columns), 0) < 14


def column_sums(ref_rows):
    return jnp.sum(ref_rows, axis=0, keepdims=True)


def reduce_kernel(slots, scalar, mask, x, *refs):
    weights, (red, stats) = refs[: 2 * slots], refs[2 * slots :]
    depth = weights[0].shape[0]
    half = weights[0].shape[1]
    for side in range(2):
        base = scalar[slots + side] * half
        for at in range(0, half, BLOCK):
            total = None
            for slot in range(slots):
                rows = pl.ds(pl.multiple_of(scalar[slot] * depth, 128), depth)
                term = dot(x[:, rows], weights[2 * slot + side][:, at : at + BLOCK])
                total = term if total is None else total + term
            columns = pl.ds(pl.multiple_of(base + at, BLOCK), BLOCK)
            red[:, columns] = total
            masked = total * mask[...]
            stats[0:1, columns] = column_sums(masked)
            stats[1:2, columns] = column_sums(masked * total)


def fill_pads(pads, image, line, values):
    rows = pl.ds(pl.multiple_of((line + 1) * LINE, LINE), LINE)
    pads[0, image, rows, :] = pltpu.roll(values, 1, 0).astype(BF16)
    pads[1, image, rows, :] = values.astype(BF16)
    pads[2, image, rows, :] = pltpu.roll(values, LINE - 1, 0).astype(BF16)


def clear_pads(pads):
    images, rows, columns = pads.shape[1:]
    zeros = jnp.zeros((3, images, LINE, columns), BF16)
    pads[:, :, 0:LINE, :] = zeros
    pads[:, :, rows - LINE : rows, :] = zeros


def group_kernel(side, mask, red, total, pixels, gain, shift, wide, pads, grouped, stats):
    images, padded, width = pads.shape[1:]
    rows = side * LINE
    mean, inverse = moments(total, pixels[...])
    scale = inverse * gain[...]
    clear_pads(pads)
    inside = line_mask(width)

    def body(step, carry):
        image, line = step // side, step % side
        at = pl.ds(pl.multiple_of(step * LINE, LINE), LINE)
        normal = (red[at, :] - mean) * scale + shift[...]
        fill_pads(pads, image, line, jnp.where(inside, normal * sigmoid(normal), 0.0))
        return carry

    lax.fori_loop(0, images * side, body, 0)
    for block in range(width // BLOCK):
        columns = slice(block * BLOCK, (block + 1) * BLOCK)
        sums = [0.0, 0.0]
        for image in range(images):
            value = None
            for tap in range(TAPS):
                top, left = divmod(tap, 3)
                term = dot(
                    pads[left, image, top * LINE : top * LINE + rows, columns], wide[tap, block]
                )
                value = term if value is None else value + term
            at = slice(image * rows, (image + 1) * rows)
            grouped[at, columns] = value
            masked = value * mask[at, :]
            sums = [sums[0] + column_sums(masked), sums[1] + column_sums(masked * value)]
        stats[0:1, columns] = sums[0]
        stats[1:2, columns] = sums[1]


def expand_kernel(scalar, mask, grouped, total, pixels, gain, shift, mine, other, act, expanded, stats):
    width = grouped.shape[1]
    mean, inverse = moments(total, pixels[...])
    scale = inverse * gain[...]
    inside = line_mask(width)

    def body(step, carry):
        at = pl.ds(pl.multiple_of(step * LINE, LINE), LINE)
        normal = (grouped[at, :] - mean) * scale + shift[...]
        act[at, :] = jnp.where(inside, normal * sigmoid(normal), 0.0).astype(BF16)
        return carry

    lax.fori_loop(0, grouped.shape[0] // LINE, body, 0)
    half = mine.shape[1]
    for side, weight in enumerate((mine, other)):
        base = scalar[side] * half
        for at in range(0, half, BLOCK):
            value = dot(act[...], weight[:, at : at + BLOCK])
            columns = pl.ds(pl.multiple_of(base + at, BLOCK), BLOCK)
            expanded[:, columns] = value
            masked = value * mask[...]
            stats[0:1, columns] = column_sums(masked)
            stats[1:2, columns] = column_sums(masked * value)


def output_kernel(side, valid, expanded, total, pixels, gain, shift, x, cotangent, output, grad, stats):
    mean, inverse = moments(total, pixels[0:1, 0:1])
    zero = jnp.zeros((8, expanded.shape[1]), F32)

    def body(step, carry):
        image, line = step // side, step % side
        at = pl.ds(pl.multiple_of(step * LINE, LINE), LINE)
        keep = valid[image].astype(F32)
        normed = (expanded[at, :] - mean) * inverse
        summed = normed * gain[...] + shift[...] + x[at, :].astype(F32)
        sigma = sigmoid(summed)
        output[image, line] = (summed * sigma * keep).astype(BF16)[0:side]
        here = cotangent[at, :].astype(F32) * keep * (sigma * (1.0 + summed * (1.0 - sigma)))
        grad[at, :] = here
        both = here * normed
        return carry[0] + here[0:8] + here[8:16], carry[1] + both[0:8] + both[8:16]

    first, second = lax.fori_loop(0, expanded.shape[0] // LINE, body, (zero, zero))
    stats[0:1, :] = column_sums(first)
    stats[1:2, :] = column_sums(second)


def back_expand_kernel(
    scalar, mask, grad, expanded, total, sums, pixels, gain, grouped, total_two, gain_two, shift_two, mine, other,
    flat, dz, stats,
):
    width = grouped.shape[1]
    mean, inverse = moments(total, pixels[0:1, 0:1])
    scale = inverse * gain[...]
    first, second = sums[0:1, :] / pixels[0:1, 0:1], sums[1:2, :] / pixels[0:1, 0:1]

    def body(step, carry):
        at = pl.ds(pl.multiple_of(step * LINE, LINE), LINE)
        normed = (expanded[at, :] - mean) * inverse
        flat[at, :] = (scale * (grad[at, :] - mask[at, :] * (first + normed * second))).astype(BF16)
        return carry

    lax.fori_loop(0, grouped.shape[0] // LINE, body, 0)
    half = mine.shape[1]
    for at in range(0, width, BLOCK):
        value = None
        for side, weight in enumerate((mine, other)):
            columns = pl.ds(pl.multiple_of(scalar[side] * half, 128), half)
            term = dot(flat[:, columns], weight[at : at + BLOCK, :], NT)
            value = term if value is None else value + term
        dz[:, at : at + BLOCK] = value
    mean_two, inverse_two = moments(total_two, pixels[...])
    zero = jnp.zeros((8, width), F32)

    def tail(step, carry):
        at = pl.ds(pl.multiple_of(step * LINE, LINE), LINE)
        normed = (grouped[at, :] - mean_two) * inverse_two
        here = dz[at, :] * dsilu(normed * gain_two[...] + shift_two[...])
        dz[at, :] = here
        both = here * normed
        return carry[0] + here[0:8] + here[8:16], carry[1] + both[0:8] + both[8:16]

    one, two = lax.fori_loop(0, grouped.shape[0] // LINE, tail, (zero, zero))
    stats[0:1, :] = column_sums(one)
    stats[1:2, :] = column_sums(two)


def weight_expand_kernel(scalar, act, flat, send, keep):
    half = send.shape[1]
    turned = act[...].T
    for side, out in enumerate((keep, send)):
        base = scalar[side] * half
        for at in range(0, half, BLOCK):
            columns = pl.ds(pl.multiple_of(base + at, BLOCK), BLOCK)
            out[:, at : at + BLOCK] = dot(turned, flat[:, columns]).astype(BF16)


def back_group_kernel(
    side, mask, dz, grouped, total, sums, pixels, gain, red, total_one, gain_one, shift_one, wide,
    flat, dz_one, stats, pads,
):
    images, padded, width = pads.shape[1:]
    rows = side * LINE
    mean, inverse = moments(total, pixels[...])
    scale = inverse * gain[...]
    first, second = sums[0:1, :] / pixels[...], sums[1:2, :] / pixels[...]
    clear_pads(pads)

    def body(step, carry):
        image, line = step // side, step % side
        at = pl.ds(pl.multiple_of(step * LINE, LINE), LINE)
        normed = (grouped[at, :] - mean) * inverse
        value = scale * (dz[at, :] - mask[at, :] * (first + normed * second))
        flat[at, :] = value.astype(BF16)
        fill_pads(pads, image, line, value)
        return carry

    lax.fori_loop(0, images * side, body, 0)
    for block in range(width // BLOCK):
        columns = slice(block * BLOCK, (block + 1) * BLOCK)
        for image in range(images):
            value = None
            for tap in range(TAPS):
                top, left = divmod(TAPS - 1 - tap, 3)
                term = dot(
                    pads[left, image, top * LINE : top * LINE + rows, columns], wide[tap, block], NT
                )
                value = term if value is None else value + term
            dz_one[image * rows : (image + 1) * rows, columns] = value
    mean_one, inverse_one = moments(total_one, pixels[...])
    inside = line_mask(width)
    zero = jnp.zeros((8, width), F32)

    def tail(step, carry):
        at = pl.ds(pl.multiple_of(step * LINE, LINE), LINE)
        normed = (red[at, :] - mean_one) * inverse_one
        here = dz_one[at, :] * dsilu(normed * gain_one[...] + shift_one[...])
        here = jnp.where(inside, here, 0.0)
        dz_one[at, :] = here
        both = here * normed
        return carry[0] + here[0:8] + here[8:16], carry[1] + both[0:8] + both[8:16]

    one, two = lax.fori_loop(0, images * side, tail, (zero, zero))
    stats[0:1, :] = column_sums(one)
    stats[1:2, :] = column_sums(two)


def weight_group_kernel(side, pads, flat, out):
    images, padded, width = pads.shape[1:]
    rows = side * LINE
    inner = width // GROUPS
    row = lax.broadcasted_iota(jnp.int32, (BLOCK, BLOCK), 0) // inner
    column = lax.broadcasted_iota(jnp.int32, (BLOCK, BLOCK), 1) // inner
    own = row == column
    fold_row = lax.broadcasted_iota(jnp.int32, (inner, BLOCK), 0)
    fold_column = lax.broadcasted_iota(jnp.int32, (inner, BLOCK), 1) % inner
    fold = jnp.where(fold_row == fold_column, 1.0, 0.0).astype(BF16)
    for block in range(width // BLOCK):
        columns = slice(block * BLOCK, (block + 1) * BLOCK)
        turned = [flat[image * rows : (image + 1) * rows, columns].T for image in range(images)]
        for tap in range(TAPS):
            top, left = divmod(tap, 3)
            value = None
            for image in range(images):
                term = dot(turned[image], pads[left, image, top * LINE : top * LINE + rows, columns])
                value = term if value is None else value + term
            kept = jnp.where(own, value, 0.0).astype(BF16)
            out[tap * inner : (tap + 1) * inner, columns] = dot(fold, kept, NT).astype(BF16)


def back_reduce_kernel(scalar, mask, dz, red, total, sums, pixels, gain, turned, flat, send, keep):
    mean, inverse = moments(total, pixels[...])
    scale = inverse * gain[...]
    first, second = sums[0:1, :] / pixels[...], sums[1:2, :] / pixels[...]

    def body(step, carry):
        at = pl.ds(pl.multiple_of(step * LINE, LINE), LINE)
        normed = (red[at, :] - mean) * inverse
        flat[at, :] = (scale * (dz[at, :] - mask[at, :] * (first + normed * second))).astype(BF16)
        return carry

    lax.fori_loop(0, red.shape[0] // LINE, body, 0)
    half = send.shape[1]
    for side, out in enumerate((keep, send)):
        base = scalar[side] * half
        for at in range(0, half, BLOCK):
            columns = pl.ds(pl.multiple_of(base + at, BLOCK), BLOCK)
            out[:, at : at + BLOCK] = dot(turned[...], flat[:, columns]).astype(BF16)


def grad_input_kernel(slots, side, scalar, flat, grad, *refs):
    weights, (out, held) = refs[: 2 * slots], refs[2 * slots :]
    depth, half = weights[0].shape
    for slot in range(slots):
        value = None
        for part in range(2):
            columns = pl.ds(pl.multiple_of(scalar[slots + part] * half, 128), half)
            term = dot(flat[:, columns], weights[2 * slot + part][...], NT)
            value = term if value is None else value + term
        columns = pl.ds(pl.multiple_of(scalar[slot] * depth, 128), depth)
        held[:, columns] = value + grad[:, columns]

    def body(step, carry):
        at = pl.ds(pl.multiple_of(step * LINE, LINE), LINE)
        out[step // side, step % side] = held[at, :].astype(BF16)[0:side]
        return carry

    lax.fori_loop(0, flat.shape[0] // LINE, body, 0)


def everywhere(values):
    values = values + lax.ppermute(values, "core", SWAP)
    chips = lax.axis_size("fsdp") * lax.axis_size("x")
    spread = jnp.broadcast_to(values[None], (chips,) + values.shape)
    return jnp.sum(lax.all_to_all(spread, ("fsdp", "x"), 0, 0, tiled=True), axis=0)


def swap_core(values):
    return lax.ppermute(values, "core", SWAP)


def around(values):
    return lax.ppermute(values, "fsdp", [(f, (f + 2) % 8) for f in range(8)])


def across(values):
    return lax.ppermute(values, "fsdp", [(f, f ^ 1) for f in range(8)])


def gather_reduce(half):
    position = lax.axis_index("fsdp")
    size = lax.axis_size("fsdp")
    if size != 8:
        return [lax.all_gather(half, "fsdp", axis=0, tiled=True)], jnp.zeros((1,), jnp.int32)
    blocks, owners, moving = [], [], half
    for step in range(4):
        if step > 0:
            moving = around(moving)
        owner = (position - 2 * step + 8) % 8
        blocks += [moving, across(moving)]
        owners += [owner, owner ^ 1]
    return blocks, jnp.stack(owners).astype(jnp.int32)


def scatter_reduce(part):
    position = lax.axis_index("fsdp")
    size = lax.axis_size("fsdp")
    if size != 8:
        flat = part.reshape(-1, part.shape[-1])
        own = lax.psum_scatter(flat, "fsdp", scatter_dimension=0, tiled=True)
        return lax.psum(own.astype(F32), "x")

    def block(owner):
        return lax.dynamic_index_in_dim(part, owner, 0, keepdims=False)

    total = None
    for step in range(1, 5):
        owner = (position - 2 * step + 8) % 8
        sent = across(block(owner ^ 1))
        here = block(owner).astype(F32) + sent.astype(F32)
        if total is not None:
            here = here + total.astype(F32)
        if step < 4:
            total = around(here.astype(BF16))
    return here + lax.ppermute(here.astype(BF16), "x", SWAP).astype(F32)


def halves(values, core):
    half = values.shape[1] // 2
    return lax.dynamic_slice_in_dim(values, core * half, half, 1)


def join(mine, other, core):
    first = jnp.where(core == 0, mine, other)
    second = jnp.where(core == 0, other, mine)
    return jnp.concatenate([first, second], axis=1)


def per_device(
    images,
    valid,
    cotangent,
    w_reduce,
    gain_one,
    shift_one,
    w_group,
    gain_two,
    shift_two,
    w_expand,
    gain_three,
    shift_three,
):
    count, side, _, channels = images.shape
    width = w_reduce.shape[1]
    inner = width // GROUPS
    size = lax.axis_size("fsdp")
    position, core = lax.axis_index("fsdp"), lax.axis_index("core").astype(jnp.int32)
    rows = count * side * LINE

    def padded(values):
        return jnp.pad(values, ((0, 0), (0, 0), (0, LINE - side), (0, 0))).reshape(rows, channels)

    x, cot = padded(images), padded(cotangent)
    turned = x.T
    pixel = jnp.arange(LINE) < side
    mask = (valid.astype(F32)[:, None, None] * pixel[None, None, :].astype(F32)) * jnp.ones((1, side, 1), F32)
    mask = mask.reshape(rows, 1)

    cores = jnp.stack([core, 1 - core])
    blocks, owners = gather_reduce(halves(w_reduce, core))
    weights = []
    for block in blocks:
        weights += [block, swap_core(block)]
    slots = jnp.concatenate([owners, cores])
    slot_count = len(blocks)
    vectors = jnp.concatenate([gain_one, shift_one, gain_two, shift_two, gain_three, shift_three])
    small = jnp.concatenate([w_group.reshape(-1), vectors])
    small = lax.all_gather(small.reshape(1, -1), "fsdp", axis=0, tiled=True)
    w_group_all = small[:, : w_group.size].reshape(TAPS, inner, width)
    vectors = small[:, w_group.size :].astype(F32)
    cut, per, outer = [], gain_one.shape[0], gain_three.shape[0]
    for begin, length in (
        (0, per), (per, per), (2 * per, per), (3 * per, per), (4 * per, outer), (4 * per + outer, outer)
    ):
        cut.append(vectors[:, begin : begin + length].reshape(1, -1))
    g1, s1, g2, s2, g3, s3 = cut
    per_block = BLOCK // inner
    tiled = jnp.broadcast_to(
        w_group_all.reshape(TAPS, 1, 1, inner, width // BLOCK, BLOCK),
        (TAPS, 1, per_block, inner, width // BLOCK, BLOCK),
    )
    tiled = tiled.reshape(TAPS, BLOCK, width // BLOCK, BLOCK).transpose(0, 2, 1, 3)
    own = (jnp.arange(BLOCK) // inner)[:, None] == (jnp.arange(BLOCK) // inner)[None, :]
    wide = jnp.where(own[None, None], tiled, jnp.zeros((), BF16))
    expand_mine = lax.all_gather(halves(w_expand, core), "fsdp", axis=0, tiled=True)
    expand_other = swap_core(expand_mine)

    red, part = call(
        functools.partial(reduce_kernel, slot_count),
        [shape((rows, width), F32), shape((2, width), F32)],
        slots, mask, x, *weights, scalars=1, name="reduce", flops=2 * rows * width * channels,
    )
    pixel_count = jnp.sum(valid.astype(F32)) * (side * side)
    part = jnp.concatenate([part, jnp.full((1, width), 1.0, F32) * pixel_count], axis=0)
    total = everywhere(part)
    total_one, pixels = total[0:2], total[2:3]
    pads, grouped, part = call(
        functools.partial(group_kernel, side),
        [
            shape((3, count, (side + 2) * LINE, width), BF16),
            shape((rows, width), F32),
            shape((2, width), F32),
        ],
        mask, red, total_one, pixels, g1, s1, wide, name="group", flops=2 * TAPS * rows * width * BLOCK,
    )
    total_two = everywhere(part)
    act_two, expanded, part = call(
        expand_kernel,
        [shape((rows, width), BF16), shape((rows, channels), F32), shape((2, channels), F32)],
        cores, mask, grouped, total_two, pixels, g2, s2, expand_mine, expand_other,
        scalars=1, name="expand", flops=2 * rows * width * channels,
    )
    total_three = everywhere(part)
    output, grad_summed, part = call(
        functools.partial(output_kernel, side),
        [shape(images.shape, BF16), shape((rows, channels), F32), shape((2, channels), F32)],
        valid, expanded, total_three, pixels, g3, s3, x, cot, scalars=1, name="output",
    )

    sums_three = everywhere(part)
    flat_three, dz_two, part = call(
        back_expand_kernel,
        [shape((rows, channels), BF16), shape((rows, width), F32), shape((2, width), F32)],
        cores, mask, grad_summed, expanded, total_three, sums_three, pixels, g3, grouped, total_two, g2, s2,
        expand_mine, expand_other, scalars=1, name="back_expand", flops=2 * rows * width * channels,
    )
    send, keep = call(
        weight_expand_kernel,
        [shape((width, channels // 2), BF16)] * 2,
        cores, act_two, flat_three, scalars=1, name="weight_expand", flops=2 * rows * width * channels,
    )
    chip = (keep.astype(F32) + swap_core(send).astype(F32)).astype(BF16)
    own_expand = lax.psum_scatter(chip, "fsdp", scatter_dimension=0, tiled=True)
    own_expand = own_expand.astype(F32)
    if lax.axis_size("x") == 2:
        own_expand = own_expand + lax.ppermute(own_expand.astype(BF16), "x", SWAP).astype(F32)
    else:
        own_expand = lax.psum(own_expand, "x")
    grad_w_expand = join(own_expand, swap_core(own_expand), core)

    sums_two = everywhere(part)
    flat_two, dz_one, part = call(
        functools.partial(back_group_kernel, side),
        [shape((rows, width), BF16), shape((rows, width), F32), shape((2, width), F32)],
        mask, dz_two, grouped, total_two, sums_two, pixels, g2, red, total_one, g1, s1, wide,
        scratch=[pltpu.VMEM((3, count, (side + 2) * LINE, width), BF16)],
        name="back_group", flops=2 * TAPS * rows * width * BLOCK,
    )
    group_term = call(
        functools.partial(weight_group_kernel, side),
        shape((TAPS * inner, width), BF16),
        pads, flat_two, name="weight_group", flops=2 * TAPS * rows * width * BLOCK,
    )
    own_group = lax.psum(group_term, ("fsdp", "x", "core"))
    shard = w_group.shape[0]
    grad_w_group = lax.dynamic_slice_in_dim(own_group, position * shard, shard, 0).astype(F32)

    sums_one = everywhere(part)
    flat_one, send, keep = call(
        back_reduce_kernel,
        [shape((rows, width), BF16)] + [shape((channels, width // 2), BF16)] * 2,
        cores, mask, dz_one, red, total_one, sums_one, pixels, g1, turned,
        scalars=1, name="back_reduce", flops=2 * rows * width * channels,
    )
    chip = (keep.astype(F32) + swap_core(send).astype(F32)).astype(BF16)
    own_reduce = scatter_reduce(chip.reshape(size, channels // size, width // 2))
    grad_w_reduce = join(own_reduce, swap_core(own_reduce), core)
    grad_input = call(
        functools.partial(grad_input_kernel, slot_count, side),
        shape(images.shape, BF16),
        slots, flat_one, grad_summed, *weights,
        scalars=1, scratch=[pltpu.VMEM((rows, channels), F32)], name="grad_input",
        flops=2 * rows * width * channels,
    )

    def own_shard(total, shard):
        return lax.dynamic_slice_in_dim(total, position * shard, shard, 0)

    return (
        output,
        grad_input,
        grad_w_reduce,
        grad_w_group,
        grad_w_expand,
        own_shard(sums_one[1], per),
        own_shard(sums_one[0], per),
        own_shard(sums_two[1], per),
        own_shard(sums_two[0], per),
        own_shard(sums_three[1], outer),
        own_shard(sums_three[0], outer),
    )


def solution(mesh):
    fsdp, dp = mesh.shape["fsdp"], mesh.shape["dp"]
    split = Mesh(mesh.devices.reshape(fsdp, dp // 2, 2), ("fsdp", "x", "core"))
    images, rows, vector = P(("fsdp", "x", "core"), None, None, None), P("fsdp", None), P("fsdp")
    return jax.shard_map(
        per_device,
        mesh=split,
        in_specs=(
            images, P(("fsdp", "x", "core")), images,
            rows, vector, vector, rows, vector, vector, rows, vector, vector,
        ),
        out_specs=(images, images, rows, rows, rows) + (vector,) * 6,
        check_vma=False,
    )
```

time: 1090 us -> 526 us (0.48)
  blocking collectives: 429 us -> 59.2 us
  local copies, waits for them, and re-layouts: 337 us -> 79.9 us
  waiting for transfers between devices: 128 us -> 240 us
  matrix products: 106 us -> 0 us
  Pallas kernels: 0 us -> 58.2 us
  starting transfers between devices: 2.27 us -> 35.9 us
  other arithmetic: 60.5 us -> 27 us
    psum x6 -> x0, blocking collectives: 243 us -> none  [the longest x3 124 us: norm_backward(): lax.psum((jnp.sum(masked, axis=(0, 1, 2)), jnp.sum(masked * normed, axis=...]
    another operation x29 -> x0, local copies, waits for them, and re-layouts: 141 us -> none
    all_gather x7 -> x1, blocking collectives: 142 us -> 34.2 us  [per_device(): small = lax.all_gather(small.reshape(1, -1), 'fsdp', axis=0, tiled=True)]
    dot_general x17 -> x0, matrix products: 106 us -> none  [the longest x9 36 us: per_device(): jnp.einsum('nhwgo,igo->nhwgi', grouped_grad, kernel[tap_index], preferred...]
    scatter-add x9 -> x0, local copies, waits for them, and re-layouts: 88.3 us -> none  [per_device(): grad_padded.at[:, vertical:vertical + side, lateral:lateral + side]]
    reduce_scatter x2 -> x1, waiting for transfers between devices: 87.1 us -> 3.43 us  [per_device(): own_expand = lax.psum_scatter(chip, 'fsdp', scatter_dimension=0, tiled=True)]
    psum x1, waiting for transfers between devices: 38.6 us -> 119 us  [per_device(): own_group = lax.psum(group_term, ('fsdp', 'x', 'core'))]
    ppermute x0 -> x35, waiting for transfers between devices: none -> 63.8 us  [the longest x6 42.3 us: around(): return lax.ppermute(values, 'fsdp', [(f, (f + 2) % 8) for f in range(8)])]
  transfers between devices with their start and end apart: 6 -> 42, of which waited for: 3 -> 21; matrix products, arithmetic and copies ran while one was open for 48% -> 11% of each run, Pallas kernels for 0% -> 7%
where the time goes in v1:
time: 526 us; the launch traced here: 516 us
  waiting for transfers between devices  240 us (46%)
  local copies, waits for them, and re-layouts  79.9 us (15%)
  blocking collectives  59.2 us (11%)
  Pallas kernels  58.2 us (11%)
  starting transfers between devices  35.9 us (7%)
  other arithmetic  27 us (5%)
  between operations  15.7 us (3%)
    psum x1, waiting for transfers between devices, per_device(): own_group = lax.psum(group_term, ('fsdp', 'x', 'core'))  119 us
    pallas_call x10, Pallas kernels, call(): pl.pallas_call(kernel, out_shape=outs, in_specs=[sm] * scalars + [vm] * (...  58.2 us
    unnamed x143, local copies, waits for them, and re-layouts  58 us
    ppermute x6, waiting for transfers between devices, around(): return lax.ppermute(values, 'fsdp', [(f, (f + 2) % 8) for f in range(8)])  42.3 us
    all_gather x1, blocking collectives, per_device(): small = lax.all_gather(small.reshape(1, -1), 'fsdp', axis=0, tiled=True)  34.2 us
    all_to_all x4, waiting for transfers between devices, everywhere(): lax.all_to_all(spread, ('fsdp', 'x'), 0, 0, tiled=True)  29.7 us
    all_to_all x2, blocking collectives, everywhere(): lax.all_to_all(spread, ('fsdp', 'x'), 0, 0, tiled=True)  25 us
    all_gather x1, waiting for transfers between devices, per_device(): lax.all_gather(halves(w_expand, core), 'fsdp', axis=0, tiled=True)  24 us
  transfers between devices with their start and end apart: 42, of which 21 were waited for; matrix products, arithmetic and copies ran while one was open for 11% of the time, Pallas kernels for 7%

profile of v1, /device:TPU:0, one launch (start us, length us, event | category | flops | bytes accessed | tf_op | source)
XLA Modules:
  0.0 516.1 jit_solution(9600116882425746750)
XLA Ops:
  10.0 3.1 collective-permute-start.3
  13.0 1.5 collective-permute-start.1
  14.6 6.8 %collective-permute-done.3.refs_4_ = bf16[256,512]{1,0:T(8,128)(2,1)S(1)} collective-permute-done((bf16[256,512]{1,0:T(8,128)(2,1)S(1)}, bf16[256,512]{1,0:T(8,128)(2,1)S(1)}, u32[]{:S(2)}, u32[]{:S(2)}) %collective-permute-start.3) | collective-permute-done | bytes 262176 | tf_op jit(solution)/shard_map/ppermute | solution.py:361
  22.3 1.6 collective-permute-start.5
  24.1 12.2 %collective-permute-done.7.refs_8_ = bf16[256,512]{1,0:T(8,128)(2,1)S(1)} collective-permute-done((bf16[256,512]{1,0:T(8,128)(2,1)S(1)}, bf16[256,512]{1,0:T(8,128)(2,1)S(1)}, u32[]{:S(2)}, u32[]{:S(2)}) %collective-permute-start.7) | collective-permute-done | bytes 262176 | tf_op jit(solution)/shard_map/ppermute | solution.py:361
  38.6 6.2 %collective-permute-done.11.refs_12_ = bf16[256,512]{1,0:T(8,128)(2,1)} collective-permute-done((bf16[256,512]{1,0:T(8,128)(2,1)S(1)}, bf16[256,512]{1,0:T(8,128)(2,1)}, u32[]{:S(2)}, u32[]{:S(2)}) %collective-permute-start.11) | collective-permute-done | bytes 262176 | tf_op jit(solution)/shard_map/ppermute | solution.py:361
  46.8 24.0 %all-gather.3.cloned.1.call-done.mine = bf16[1024,1024]{1,0:T(8,128)(2,1)} async-done(((bf16[128,1024]{1,0:T(8,128)(2,1)}), bf16[1024,1024]{1,0:T(8,128)(2,1)}) %all-gather.3.cloned.1.call-update) | async-done | bytes 2097168 | tf_op jit(solution)/shard_map/all_gather | solution.py:473
  76.2 34.2 %all-gather = bf16[303104]{0:T(1024)(128)(2,1)} all-gather(bf16[37888]{0:T(1024)(128)(2,1)S(1)} %dynamic-update-slice.6), channel_id=2, replica_groups=mesh['fsdp'=8,'x'=2,'core'=2] {'fsdp'}, dimensions={0}, use_global_device_ids=true | all-gather | bytes 681984 | tf_op jit(solution)/shard_map/all_gather | solution.py:456
  111.7 3.6 reduce.1
  116.7 2.1 reshape.187
  118.9 1.9 slice.69
  120.8 2.3 broadcast_in_dim.32
  124.3 2.4 bitcast_select_fusion
  127.5 4.9 all-to-all-start
  133.2 9.8 %all-to-all-done = f32[16,3,1024]{2,1,0:T(4,128)S(1)} async-done(((f32[16,3,1024]{2,1,0:T(4,128)}), f32[16,3,1024]{2,1,0:T(4,128)S(1)}, u32[]{:S(2)}, u32[]{:S(2)}) %all-to-all-start) | async-done | bytes 196640 | tf_op jit(solution)/shard_map/all_to_all | solution.py:353
  143.0 2.3 copy-done.2
  146.9 3.4 group.1
  151.6 1.6 copy-done.51
  155.1 3.7 all-to-all-start.1
  158.9 7.9 %all-to-all-done.1 = f32[16,2,1024]{2,1,0:T(2,128)S(1)} async-done(((f32[16,2,1024]{2,1,0:T(2,128)}), f32[16,2,1024]{2,1,0:T(2,128)S(1)}, u32[]{:S(2)}, u32[]{:S(2)}) %all-to-all-start.1) | async-done | bytes 131104 | tf_op jit(solution)/shard_map/all_to_all | solution.py:353
  168.3 1.6 copy-done.17
  169.9 4.8 expand.1
  174.8 1.9 copy-done.4
  179.6 3.5 all-to-all-start.2
  183.2 2.1 copy.92
  185.3 1.5 pad.9.clone
  186.8 6.7 %all-to-all-done.2 = f32[16,2,2048]{2,1,0:T(2,128)S(1)} async-done(((f32[16,2,2048]{2,1,0:T(2,128)}), f32[16,2,2048]{2,1,0:T(2,128)S(1)}, u32[]{:S(2)}, u32[]{:S(2)}) %all-to-all-start.2) | async-done | bytes 262176 | tf_op jit(solution)/shard_map/all_to_all | solution.py:353
  193.7 2.0 copy-done.5
  197.2 4.0 output.1
  201.3 1.9 copy-done.6
  205.7 13.7 %all_to_all.30 = f32[16,2,2048]{2,1,0:T(2,128)} all-to-all(f32[16,2,2048]{2,1,0:T(2,128)S(1)} %broadcast_in_dim.38), channel_id=1, replica_groups=mesh['fsdp'=8,'x'=2,'core'=2] {'fsdp','x'}, dimensions={0} | all-to-all | bytes 524288 | tf_op jit(solution)/shard_map/all_to_all | solution.py:353
  220.5 2.0 copy-done.7
  224.0 1.6 copy-done.18
  225.6 9.0 %back_expand.1 = (bf16[448,2048]{1,0:T(8,128)(2,1)S(1)}, f32[448,1024]{1,0:T(8,128)S(1)}, f32[2,1024]{1,0:T(2,128)S(1)}) custom-call(s32[2]{0:T(128)S(1)} %pad_add_fusion.1.scalar, f32[448,1]{1,0:T(8,128)S(1)} %reshape.188.mask, f32[448,2048]{1,0:T(8,128)S(1)} %copy-done.7, f32[448,2048]{1,0:T(8,128)} %copy-done.4, f32[2,2048]{1,0:T(2,128)S(1)} %reduce_sum.66.total, ...), custom_call_target="tpu_custom_call" | custom-call | flops 1879048192 | bytes 1048576 | tf_op jit(solution)/shard_map/back_expand/pallas_call | solution.py:41
  234.6 4.3 weight_expand.1
  240.7 3.3 collective-permute-done.20
  244.0 11.3 %all_to_all.31 = f32[16,2,1024]{2,1,0:T(2,128)S(1)} all-to-all(f32[16,2,1024]{2,1,0:T(2,128)S(1)} %broadcast_in_dim.39), channel_id=1, replica_groups=mesh['fsdp'=8,'x'=2,'core'=2] {'fsdp','x'}, dimensions={0} | all-to-all | bytes 262144 | tf_op jit(solution)/shard_map/all_to_all | solution.py:353
  255.4 2.3 copy-done.3
  262.2 7.2 %back_group.1 = (bf16[448,1024]{1,0:T(8,128)(2,1)S(1)}, f32[448,1024]{1,0:T(8,128)S(1)}, f32[2,1024]{1,0:T(2,128)S(1)}) custom-call(f32[448,1]{1,0:T(8,128)S(1)} %reshape.188.mask, f32[448,1024]{1,0:T(8,128)S(1)} %copy-done.26, f32[448,1024]{1,0:T(8,128)S(1)} %copy-done.13, f32[2,1024]{1,0:T(2,128)S(1)} %reduce_sum.65.total.total_two, ...), custom_call_target="tpu_custom_call" | custom-call | flops 2113929216 | bytes 1048576 | tf_op jit(solution)/shard_map/back_group/pallas_call | solution.py:41
  273.5 3.5 all-to-all-start.5
  277.2 2.5 copy.80
  279.7 5.3 %all-to-all-done.5 = f32[16,2,1024]{2,1,0:T(2,128)S(1)} async-done(((f32[16,2,1024]{2,1,0:T(2,128)}), f32[16,2,1024]{2,1,0:T(2,128)S(1)}, u32[]{:S(2)}, u32[]{:S(2)}) %all-to-all-start.5) | async-done | bytes 131104 | tf_op jit(solution)/shard_map/all_to_all | solution.py:353
  285.1 1.6 copy-done.16
  289.6 6.4 %back_reduce.1 = (bf16[448,1024]{1,0:T(8,128)(2,1)S(1)}, bf16[2048,512]{1,0:T(8,128)(2,1)}, bf16[2048,512]{1,0:T(8,128)(2,1)S(1)}) custom-call(s32[2]{0:T(128)S(1)} %pad_add_fusion.1.scalar, f32[448,1]{1,0:T(8,128)S(1)} %reshape.188.mask, f32[448,1024]{1,0:T(8,128)S(1)} %copy-done.48, f32[448,1024]{1,0:T(8,128)S(1)} %copy-done.24, ...), custom_call_target="tpu_custom_call" | custom-call | flops 1879048192 | bytes 1048576 | tf_op jit(solution)/shard_map/back_reduce/pallas_call | solution.py:41
  297.0 3.9 add_convert_fusion
  301.5 3.5 add_convert_fusion.1
  305.1 2.3 dynamic-slice_bitcast_fusion.3
  309.4 7.4 %collective-permute-done.26 = bf16[256,512]{1,0:T(8,128)(2,1)} collective-permute-done((bf16[256,512]{1,0:T(8,128)(2,1)}, bf16[256,512]{1,0:T(8,128)(2,1)}, u32[]{:S(2)}, u32[]{:S(2)}) %collective-permute-start.26) | collective-permute-done | bytes 262176 | tf_op jit(solution)/shard_map/ppermute | solution.py:365
  316.8 1.8 fusion
  320.0 2.8 copy.82
  324.5 9.9 %collective-permute-done.27 = bf16[256,512]{1,0:T(8,128)(2,1)} collective-permute-done((bf16[256,512]{1,0:T(8,128)(2,1)}, bf16[256,512]{1,0:T(8,128)(2,1)}, u32[]{:S(2)}, u32[]{:S(2)}) %collective-permute-start.27) | collective-permute-done | bytes 262176 | tf_op jit(solution)/shard_map/ppermute | solution.py:361
  336.9 7.2 %collective-permute-done.28 = bf16[256,512]{1,0:T(8,128)(2,1)S(1)} collective-permute-done((bf16[256,512]{1,0:T(8,128)(2,1)S(1)}, bf16[256,512]{1,0:T(8,128)(2,1)S(1)}, u32[]{:S(2)}, u32[]{:S(2)}) %collective-permute-start.28) | collective-permute-done | bytes 262176 | tf_op jit(solution)/shard_map/ppermute | solution.py:361
  344.1 1.8 fusion.4
  346.1 11.2 %weight_group.1 = bf16[288,1024]{1,0:T(8,128)(2,1)} custom-call(bf16[3,2,256,1024]{3,2,1,0:T(8,128)(2,1)S(1)} %copy-done.52, bf16[448,1024]{1,0:T(8,128)(2,1)S(1)} %copy-done.50), custom_call_target="tpu_custom_call" | custom-call | flops 2113929216 | bytes 1048576 | tf_op jit(solution)/shard_map/weight_group/pallas_call | solution.py:41
  358.8 2.5 collective-permute-start.30
  361.9 4.5 collective-permute-done.30
  366.3 2.1 convert_add_fusion.5
  368.4 3.4 reduce-scatter.2.cloned.1.call-done
  371.8 1.5 collective-permute-start.33
  373.4 2.0 copy-done.8
  376.4 4.3 grad_input.1
  381.2 2.8 copy.83
  384.9 119.1 %all-reduce.5.cloned.1.call-done = bf16[288,1024]{1,0:T(8,128)(2,1)} async-done(((bf16[288,1024]{1,0:T(8,128)(2,1)}), bf16[288,1024]{1,0:T(8,128)(2,1)}) %all-reduce.5.cloned.1.call-update) | async-done | bytes 589840 | tf_op jit(solution)/shard_map/psum | solution.py:542
  504.0 1.6 dynamic-slice_convert_fusion
  (244 shorter events, 64.9 us)
Async XLA Ops:
  7.2 63.9 %copy-start.55 = (bf16[2,14,14,2048]{3,0,2,1:T(2,128)(2,1)S(1)}, bf16[2,14,14,2048]{3,0,2,1:T(2,128)(2,1)}, u32[]{:S(2)}) copy-start(bf16[2,14,14,2048]{3,0,2,1:T(2,128)(2,1)} %param.12) | copy-start | bytes 4816900
  7.2 63.6 %all-gather.3.cloned.1.call-start = ((), (), s32[]{:S(2)}) async-start(), calls=%async_computation.7 | async-start | bytes 2359296 | tf_op jit(solution)/shard_map/all_gather | solution.py:473
  10.0 11.4 %collective-permute-start.3 = (bf16[256,512]{1,0:T(8,128)(2,1)S(1)}, bf16[256,512]{1,0:T(8,128)(2,1)S(1)}, u32[]{:S(2)}, u32[]{:S(2)}) collective-permute-start(bf16[256,512]{1,0:T(8,128)(2,1)S(1)} %constant_dynamic-slice_fusion.7.refs_0_), channel_id=1, source_target_pairs={{0,8},{4,12},{8,16},{12,20},{16,24},{20,28},{24,0},{28,4},{1,9},{5... | collective-permute-start | bytes 786440 | tf_op jit(solution)/shard_map/ppermute | solution.py:361
  13.0 10.9 %collective-permute-start.1 = (bf16[256,512]{1,0:T(8,128)(2,1)S(1)}, bf16[256,512]{1,0:T(8,128)(2,1)S(1)}, u32[]{:S(2)}, u32[]{:S(2)}) collective-permute-start(bf16[256,512]{1,0:T(8,128)(2,1)S(1)} %constant_dynamic-slice_fusion.7.refs_0_), channel_id=1, source_target_pairs={{0,4},{4,0},{8,12},{12,8},{16,20},{20,16},{24,28},{28,24},{1,5},{5... | collective-permute-start | bytes 786440 | tf_op jit(solution)/shard_map/ppermute | solution.py:365
  21.4 14.9 %collective-permute-start.7 = (bf16[256,512]{1,0:T(8,128)(2,1)S(1)}, bf16[256,512]{1,0:T(8,128)(2,1)S(1)}, u32[]{:S(2)}, u32[]{:S(2)}) collective-permute-start(bf16[256,512]{1,0:T(8,128)(2,1)S(1)} %collective-permute-done.3.refs_4_), channel_id=1, source_target_pairs={{0,8},{4,12},{8,16},{12,20},{16,24},{20,28},{24,0},{28,4},{1,9},{5... | collective-permute-start | bytes 786440 | tf_op jit(solution)/shard_map/ppermute | solution.py:361
  21.4 15.7 %collective-permute-start = (bf16[256,512]{1,0:T(8,128)(2,1)S(1)}, bf16[256,512]{1,0:T(8,128)(2,1)S(1)}, u32[]{:S(2)}, u32[]{:S(2)}) collective-permute-start(bf16[256,512]{1,0:T(8,128)(2,1)S(1)} %constant_dynamic-slice_fusion.7.refs_0_), channel_id=1, source_target_pairs={{0,1},{1,0},{2,3},{3,2},{4,5},{5,4},{6,7},{7,6},{8,9},{9,8},{10,11... | collective-permute-start | bytes 786440 | tf_op jit(solution)/shard_map/ppermute | solution.py:357
  22.3 16.1 %collective-permute-start.5 = (bf16[256,512]{1,0:T(8,128)(2,1)S(1)}, bf16[256,512]{1,0:T(8,128)(2,1)}, u32[]{:S(2)}, u32[]{:S(2)}) collective-permute-start(bf16[256,512]{1,0:T(8,128)(2,1)S(1)} %collective-permute-done.3.refs_4_), channel_id=1, source_target_pairs={{0,4},{4,0},{8,12},{12,8},{16,20},{20,16},{24,28},{28,24},{1,5},{5... | collective-permute-start | bytes 786440 | tf_op jit(solution)/shard_map/ppermute | solution.py:365
  23.9 86.6 %copy-start.29 = (bf16[256,512]{1,0:T(8,128)(2,1)}, bf16[256,512]{1,0:T(8,128)(2,1)S(1)}, u32[]{:S(2)}) copy-start(bf16[256,512]{1,0:T(8,128)(2,1)S(1)} %collective-permute-done.1.refs_2_) | copy-start | bytes 786436
  23.9 22.2 %collective-permute-start.2 = (bf16[256,512]{1,0:T(8,128)(2,1)S(1)}, bf16[256,512]{1,0:T(8,128)(2,1)S(1)}, u32[]{:S(2)}, u32[]{:S(2)}) collective-permute-start(bf16[256,512]{1,0:T(8,128)(2,1)S(1)} %collective-permute-done.1.refs_2_), channel_id=1, source_target_pairs={{0,1},{1,0},{2,3},{3,2},{4,5},{5,4},{6,7},{7,6},{8,9},{9,8},{10,11... | collective-permute-start | bytes 786440 | tf_op jit(solution)/shard_map/ppermute | solution.py:357
  36.3 74.2 %copy-start.31 = (bf16[256,512]{1,0:T(8,128)(2,1)}, bf16[256,512]{1,0:T(8,128)(2,1)S(1)}, u32[]{:S(2)}) copy-start(bf16[256,512]{1,0:T(8,128)(2,1)S(1)} %collective-permute-done.7.refs_8_) | copy-start | bytes 786436
  36.3 8.5 %collective-permute-start.11 = (bf16[256,512]{1,0:T(8,128)(2,1)S(1)}, bf16[256,512]{1,0:T(8,128)(2,1)}, u32[]{:S(2)}, u32[]{:S(2)}) collective-permute-start(bf16[256,512]{1,0:T(8,128)(2,1)S(1)} %collective-permute-done.7.refs_8_), channel_id=1, source_target_pairs={{0,8},{4,12},{8,16},{12,20},{16,24},{20,28},{24,0},{28,4},{1,9},{5... | collective-permute-start | bytes 786440 | tf_op jit(solution)/shard_map/ppermute | solution.py:361
  37.0 38.0 %collective-permute-start.4 = (bf16[256,512]{1,0:T(8,128)(2,1)S(1)}, bf16[256,512]{1,0:T(8,128)(2,1)}, u32[]{:S(2)}, u32[]{:S(2)}) collective-permute-start(bf16[256,512]{1,0:T(8,128)(2,1)S(1)} %collective-permute-done.3.refs_4_), channel_id=1, source_target_pairs={{0,1},{1,0},{2,3},{3,2},{4,5},{5,4},{6,7},{7,6},{8,9},{9,8},{10,11... | collective-permute-start | bytes 786440 | tf_op jit(solution)/shard_map/ppermute | solution.py:357
  37.0 73.5 %copy-start.33 = (bf16[256,512]{1,0:T(8,128)(2,1)}, bf16[256,512]{1,0:T(8,128)(2,1)S(1)}, u32[]{:S(2)}) copy-start(bf16[256,512]{1,0:T(8,128)(2,1)S(1)} %collective-permute-done.refs_1_) | copy-start | bytes 786436
  37.1 38.7 %collective-permute-start.9 = (bf16[256,512]{1,0:T(8,128)(2,1)S(1)}, bf16[256,512]{1,0:T(8,128)(2,1)}, u32[]{:S(2)}, u32[]{:S(2)}) collective-permute-start(bf16[256,512]{1,0:T(8,128)(2,1)S(1)} %collective-permute-done.7.refs_8_), channel_id=1, source_target_pairs={{0,4},{4,0},{8,12},{12,8},{16,20},{20,16},{24,28},{28,24},{1,5},{5... | collective-permute-start | bytes 786440 | tf_op jit(solution)/shard_map/ppermute | solution.py:365
  38.4 37.2 %collective-permute-start.6 = (bf16[256,512]{1,0:T(8,128)(2,1)}, bf16[256,512]{1,0:T(8,128)(2,1)}, u32[]{:S(2)}, u32[]{:S(2)}) collective-permute-start(bf16[256,512]{1,0:T(8,128)(2,1)} %collective-permute-done.5.refs_6_), channel_id=1, source_target_pairs={{0,1},{1,0},{2,3},{3,2},{4,5},{5,4},{6,7},{7,6},{8,9},{9,8},{10,11... | collective-permute-start | bytes 786440 | tf_op jit(solution)/shard_map/ppermute | solution.py:357
  44.8 31.3 %collective-permute-start.13 = (bf16[256,512]{1,0:T(8,128)(2,1)}, bf16[256,512]{1,0:T(8,128)(2,1)}, u32[]{:S(2)}, u32[]{:S(2)}) collective-permute-start(bf16[256,512]{1,0:T(8,128)(2,1)} %collective-permute-done.11.refs_12_), channel_id=1, source_target_pairs={{0,4},{4,0},{8,12},{12,8},{16,20},{20,16},{24,28},{28,24},{1,5},{5... | collective-permute-start | bytes 786440 | tf_op jit(solution)/shard_map/ppermute | solution.py:365
  70.8 96.0 %collective-permute-start.17 = (bf16[1024,1024]{1,0:T(8,128)(2,1)}, bf16[1024,1024]{1,0:T(8,128)(2,1)}, u32[]{:S(2)}, u32[]{:S(2)}) collective-permute-start(bf16[1024,1024]{1,0:T(8,128)(2,1)} %all-gather.3.cloned.1.call-done.mine), channel_id=1, source_target_pairs={{0,1},{1,0},{2,3},{3,2},{4,5},{5,4},{6,7},{7,6},{8,9},{9,8},{10,11... | collective-permute-start | bytes 6291464 | tf_op jit(solution)/shard_map/ppermute | solution.py:357
  75.1 35.4 %collective-permute-start.8 = (bf16[256,512]{1,0:T(8,128)(2,1)S(1)}, bf16[256,512]{1,0:T(8,128)(2,1)S(1)}, u32[]{:S(2)}, u32[]{:S(2)}) collective-permute-start(bf16[256,512]{1,0:T(8,128)(2,1)S(1)} %collective-permute-done.7.refs_8_), channel_id=1, source_target_pairs={{0,1},{1,0},{2,3},{3,2},{4,5},{5,4},{6,7},{7,6},{8,9},{9,8},{10,11... | collective-permute-start | bytes 786440 | tf_op jit(solution)/shard_map/ppermute | solution.py:357
  75.6 34.9 %collective-permute-start.12 = (bf16[256,512]{1,0:T(8,128)(2,1)}, bf16[256,512]{1,0:T(8,128)(2,1)S(1)}, u32[]{:S(2)}, u32[]{:S(2)}) collective-permute-start(bf16[256,512]{1,0:T(8,128)(2,1)} %collective-permute-done.11.refs_12_), channel_id=1, source_target_pairs={{0,1},{1,0},{2,3},{3,2},{4,5},{5,4},{6,7},{7,6},{8,9},{9,8},{10,11... | collective-permute-start | bytes 786440 | tf_op jit(solution)/shard_map/ppermute | solution.py:357
  75.7 34.8 %collective-permute-start.10 = (bf16[256,512]{1,0:T(8,128)(2,1)}, bf16[256,512]{1,0:T(8,128)(2,1)S(1)}, u32[]{:S(2)}, u32[]{:S(2)}) collective-permute-start(bf16[256,512]{1,0:T(8,128)(2,1)} %collective-permute-done.9.refs_10_), channel_id=1, source_target_pairs={{0,1},{1,0},{2,3},{3,2},{4,5},{5,4},{6,7},{7,6},{8,9},{9,8},{10,11... | collective-permute-start | bytes 786440 | tf_op jit(solution)/shard_map/ppermute | solution.py:357
  76.1 34.4 %collective-permute-start.14 = (bf16[256,512]{1,0:T(8,128)(2,1)}, bf16[256,512]{1,0:T(8,128)(2,1)S(1)}, u32[]{:S(2)}, u32[]{:S(2)}) collective-permute-start(bf16[256,512]{1,0:T(8,128)(2,1)} %collective-permute-done.13.refs_14_), channel_id=1, source_target_pairs={{0,1},{1,0},{2,3},{3,2},{4,5},{5,4},{6,7},{7,6},{8,9},{9,8},{10,11... | collective-permute-start | bytes 786440 | tf_op jit(solution)/shard_map/ppermute | solution.py:357
  110.5 4.8 copy-start.38
  110.5 4.8 copy-start.42
  110.5 4.8 copy-start.40
  110.5 4.8 copy-start.44
  116.6 10.1 %collective-permute-start.15 = (f32[3,1024]{1,0:T(4,128)S(1)}, f32[3,1024]{1,0:T(4,128)S(1)}, u32[]{:S(2)}, u32[]{:S(2)}) collective-permute-start(f32[3,1024]{1,0:T(4,128)S(1)} %concatenate.17), channel_id=1, source_target_pairs={{0,1},{1,0},{2,3},{3,2},{4,5},{5,4},{6,7},{7,6},{8,9},{9,8},{10,11... | collective-permute-start | bytes 36872 | tf_op jit(solution)/shard_map/ppermute | solution.py:350
  127.5 15.5 %all-to-all-start = ((f32[16,3,1024]{2,1,0:T(4,128)}), f32[16,3,1024]{2,1,0:T(4,128)S(1)}, u32[]{:S(2)}, u32[]{:S(2)}) async-start(f32[16,3,1024]{2,1,0:T(4,128)} %broadcast_in_dim.30), calls=%async_computation | async-start | bytes 524288 | tf_op jit(solution)/shard_map/all_to_all | solution.py:353
  153.2 1.2 collective-permute-start.16
  155.1 11.7 %all-to-all-start.1 = ((f32[16,2,1024]{2,1,0:T(2,128)}), f32[16,2,1024]{2,1,0:T(2,128)S(1)}, u32[]{:S(2)}, u32[]{:S(2)}) async-start(f32[16,2,1024]{2,1,0:T(2,128)} %broadcast_in_dim.36), calls=%async_computation.1 | async-start | bytes 262144 | tf_op jit(solution)/shard_map/all_to_all | solution.py:353
  177.6 1.2 collective-permute-start.18
  179.6 14.0 %all-to-all-start.2 = ((f32[16,2,2048]{2,1,0:T(2,128)}), f32[16,2,2048]{2,1,0:T(2,128)S(1)}, u32[]{:S(2)}, u32[]{:S(2)}) async-start(f32[16,2,2048]{2,1,0:T(2,128)} %broadcast_in_dim.37), calls=%async_computation.2 | async-start | bytes 524288 | tf_op jit(solution)/shard_map/all_to_all | solution.py:353
  204.4 1.2 collective-permute-start.19
  225.6 9.0 %copy-start.54 = (bf16[448,1024]{1,0:T(8,128)(2,1)S(1)}, bf16[448,1024]{1,0:T(8,128)(2,1)}, u32[]{:S(2)}) copy-start(bf16[448,1024]{1,0:T(8,128)(2,1)} %copy-done.53) | copy-start | bytes 2752516
  234.6 4.3 copy-start.25
  240.2 56.8 %collective-permute-start.32 = (bf16[1024,1024]{1,0:T(8,128)(2,1)}, bf16[1024,1024]{1,0:T(8,128)(2,1)}, u32[]{:S(2)}, u32[]{:S(2)}) collective-permute-start(bf16[1024,1024]{1,0:T(8,128)(2,1)} %get-tuple-element.54), channel_id=1, source_target_pairs={{0,1},{1,0},{2,3},{3,2},{4,5},{5,4},{6,7},{7,6},{8,9},{9,8},{10,11... | collective-permute-start | bytes 6291464 | tf_op jit(solution)/shard_map/ppermute | solution.py:357
  240.2 3.8 collective-permute-start.20
  271.6 1.2 collective-permute-start.21
  273.5 11.5 %all-to-all-start.5 = ((f32[16,2,1024]{2,1,0:T(2,128)}), f32[16,2,1024]{2,1,0:T(2,128)S(1)}, u32[]{:S(2)}, u32[]{:S(2)}) async-start(f32[16,2,1024]{2,1,0:T(2,128)} %broadcast_in_dim.72), calls=%async_computation.5 | async-start | bytes 262144 | tf_op jit(solution)/shard_map/all_to_all | solution.py:353
  277.0 94.8 %reduce-scatter.2.cloned.1.call-start = ((), (), s32[]{:S(2)}) async-start(), calls=%async_computation.9 | async-start | bytes 2359296 | tf_op jit(solution)/shard_map/reduce_scatter | solution.py:521
  289.6 7.4 %copy-start.15 = (bf16[1024,1024]{1,0:T(8,128)(2,1)S(1)}, bf16[1024,1024]{1,0:T(8,128)(2,1)}, u32[]{:S(2)}) copy-start(bf16[1024,1024]{1,0:T(8,128)(2,1)} %copy-done.14) | copy-start | bytes 6291460
  297.0 4.5 collective-permute-start.22
  300.9 203.0 %all-reduce.5.cloned.1.call-start = ((), (), s32[]{:S(2)}) async-start(), calls=%async_computation.8 | async-start | bytes 1179648 | tf_op jit(solution)/shard_map/psum | solution.py:542
  305.1 14.9 %copy-start.20 = (bf16[2,14,14,2048]{3,2,1,0:T(8,128)(2,1)S(1)}, bf16[2,14,14,2048]{3,2,1,0:T(8,128)(2,1)}, u32[]{:S(2)}) copy-start(bf16[2,14,14,2048]{3,2,1,0:T(8,128)(2,1)} %copy-done.19) | copy-start | bytes 4816900
  307.3 9.5 %collective-permute-start.26 = (bf16[256,512]{1,0:T(8,128)(2,1)}, bf16[256,512]{1,0:T(8,128)(2,1)}, u32[]{:S(2)}, u32[]{:S(2)}) collective-permute-start(bf16[256,512]{1,0:T(8,128)(2,1)} %get-tuple-element.111), channel_id=1, source_target_pairs={{0,4},{4,0},{8,12},{12,8},{16,20},{20,16},{24,28},{28,24},{1,5},{5... | collective-permute-start | bytes 786440 | tf_op jit(solution)/shard_map/ppermute | solution.py:365
  308.0 16.5 %collective-permute-start.25 = (bf16[256,512]{1,0:T(8,128)(2,1)S(1)}, bf16[256,512]{1,0:T(8,128)(2,1)}, u32[]{:S(2)}, u32[]{:S(2)}) collective-permute-start(bf16[256,512]{1,0:T(8,128)(2,1)S(1)} %get-tuple-element.112), channel_id=1, source_target_pairs={{0,4},{4,0},{8,12},{12,8},{16,20},{20,16},{24,28},{28,24},{1,5},{5... | collective-permute-start | bytes 786440 | tf_op jit(solution)/shard_map/ppermute | solution.py:365
  318.6 15.8 %collective-permute-start.27 = (bf16[256,512]{1,0:T(8,128)(2,1)}, bf16[256,512]{1,0:T(8,128)(2,1)}, u32[]{:S(2)}, u32[]{:S(2)}) collective-permute-start(bf16[256,512]{1,0:T(8,128)(2,1)} %fusion), channel_id=1, source_target_pairs={{0,8},{4,12},{8,16},{12,20},{16,24},{20,28},{24,0},{28,4},{1,9},{5... | collective-permute-start | bytes 786440 | tf_op jit(solution)/shard_map/ppermute | solution.py:361
  320.0 26.1 %copy-start.50 = (bf16[448,1024]{1,0:T(8,128)(2,1)S(1)}, bf16[448,1024]{1,0:T(8,128)(2,1)}, u32[]{:S(2)}) copy-start(bf16[448,1024]{1,0:T(8,128)(2,1)} %copy-done.49) | copy-start | bytes 2752516
  320.0 26.1 %copy-start.52 = (bf16[3,2,256,1024]{3,2,1,0:T(8,128)(2,1)S(1)}, bf16[3,2,256,1024]{3,2,1,0:T(8,128)(2,1)}, u32[]{:S(2)}) copy-start(bf16[3,2,256,1024]{3,2,1,0:T(8,128)(2,1)} %copy-done.51) | copy-start | bytes 9437188
  322.8 14.1 %collective-permute-start.24 = (bf16[256,512]{1,0:T(8,128)(2,1)S(1)}, bf16[256,512]{1,0:T(8,128)(2,1)S(1)}, u32[]{:S(2)}, u32[]{:S(2)}) collective-permute-start(bf16[256,512]{1,0:T(8,128)(2,1)S(1)} %get-tuple-element.113), channel_id=1, source_target_pairs={{0,4},{4,0},{8,12},{12,8},{16,20},{20,16},{24,28},{28,24},{1,5},{5... | collective-permute-start | bytes 786440 | tf_op jit(solution)/shard_map/ppermute | solution.py:365
  335.6 8.5 %collective-permute-start.28 = (bf16[256,512]{1,0:T(8,128)(2,1)S(1)}, bf16[256,512]{1,0:T(8,128)(2,1)S(1)}, u32[]{:S(2)}, u32[]{:S(2)}) collective-permute-start(bf16[256,512]{1,0:T(8,128)(2,1)S(1)} %fusion.2), channel_id=1, source_target_pairs={{0,8},{4,12},{8,16},{12,20},{16,24},{20,28},{24,0},{28,4},{1,9},{5... | collective-permute-start | bytes 786440 | tf_op jit(solution)/shard_map/ppermute | solution.py:361
  336.3 21.2 %collective-permute-start.23 = (bf16[256,512]{1,0:T(8,128)(2,1)}, bf16[256,512]{1,0:T(8,128)(2,1)}, u32[]{:S(2)}, u32[]{:S(2)}) collective-permute-start(bf16[256,512]{1,0:T(8,128)(2,1)} %get-tuple-element.110), channel_id=1, source_target_pairs={{0,4},{4,0},{8,12},{12,8},{16,20},{20,16},{24,28},{28,24},{1,5},{5... | collective-permute-start | bytes 786440 | tf_op jit(solution)/shard_map/ppermute | solution.py:365
  345.9 11.6 %collective-permute-start.29 = (bf16[256,512]{1,0:T(8,128)(2,1)}, bf16[256,512]{1,0:T(8,128)(2,1)}, u32[]{:S(2)}, u32[]{:S(2)}) collective-permute-start(bf16[256,512]{1,0:T(8,128)(2,1)} %fusion.4), channel_id=1, source_target_pairs={{0,8},{4,12},{8,16},{12,20},{16,24},{20,28},{24,0},{28,4},{1,9},{5... | collective-permute-start | bytes 786440 | tf_op jit(solution)/shard_map/ppermute | solution.py:361
  357.3 16.0 %copy-start.28 = (bf16[448,1024]{1,0:T(8,128)(2,1)S(1)}, bf16[448,1024]{1,0:T(8,128)(2,1)}, u32[]{:S(2)}) copy-start(bf16[448,1024]{1,0:T(8,128)(2,1)} %copy-done.27) | copy-start | bytes 2752516
  357.3 16.0 %copy-start.30 = (bf16[256,512]{1,0:T(8,128)(2,1)S(1)}, bf16[256,512]{1,0:T(8,128)(2,1)}, u32[]{:S(2)}) copy-start(bf16[256,512]{1,0:T(8,128)(2,1)} %copy-done.29) | copy-start | bytes 786436
  357.3 16.0 %copy-start.32 = (bf16[256,512]{1,0:T(8,128)(2,1)S(1)}, bf16[256,512]{1,0:T(8,128)(2,1)}, u32[]{:S(2)}) copy-start(bf16[256,512]{1,0:T(8,128)(2,1)} %copy-done.31) | copy-start | bytes 786436
  357.3 16.0 %copy-start.34 = (bf16[256,512]{1,0:T(8,128)(2,1)S(1)}, bf16[256,512]{1,0:T(8,128)(2,1)}, u32[]{:S(2)}) copy-start(bf16[256,512]{1,0:T(8,128)(2,1)} %copy-done.33) | copy-start | bytes 786436
  357.3 16.0 %copy-start.37 = (bf16[256,512]{1,0:T(8,128)(2,1)S(1)}, bf16[256,512]{1,0:T(8,128)(2,1)}, u32[]{:S(2)}) copy-start(bf16[256,512]{1,0:T(8,128)(2,1)} %copy-done.35) | copy-start | bytes 786436
  357.3 16.0 %copy-start.39 = (bf16[256,512]{1,0:T(8,128)(2,1)S(1)}, bf16[256,512]{1,0:T(8,128)(2,1)}, u32[]{:S(2)}) copy-start(bf16[256,512]{1,0:T(8,128)(2,1)} %copy-done.38) | copy-start | bytes 786436
  357.3 16.0 %copy-start.41 = (bf16[256,512]{1,0:T(8,128)(2,1)S(1)}, bf16[256,512]{1,0:T(8,128)(2,1)}, u32[]{:S(2)}) copy-start(bf16[256,512]{1,0:T(8,128)(2,1)} %copy-done.40) | copy-start | bytes 786436
  357.4 16.0 %copy-start.43 = (bf16[256,512]{1,0:T(8,128)(2,1)S(1)}, bf16[256,512]{1,0:T(8,128)(2,1)}, u32[]{:S(2)}) copy-start(bf16[256,512]{1,0:T(8,128)(2,1)} %copy-done.42) | copy-start | bytes 786436
  358.8 7.5 %collective-permute-start.30 = (bf16[256,512]{1,0:T(8,128)(2,1)S(1)}, bf16[256,512]{1,0:T(8,128)(2,1)S(1)}, u32[]{:S(2)}, u32[]{:S(2)}) collective-permute-start(bf16[256,512]{1,0:T(8,128)(2,1)S(1)} %fusion.6), channel_id=1, source_target_pairs={{0,2},{2,0},{1,3},{3,1},{4,6},{6,4},{5,7},{7,5},{8,10},{10,8},{9,1... | collective-permute-start | bytes 786440 | tf_op jit(solution)/shard_map/ppermute | solution.py:403
  368.4 137.1 %collective-permute-start.31 = (f32[256,512]{1,0:T(8,128)}, f32[256,512]{1,0:T(8,128)}, u32[]{:S(2)}, u32[]{:S(2)}) collective-permute-start(f32[256,512]{1,0:T(8,128)} %convert_add_fusion.5), channel_id=1, source_target_pairs={{0,1},{1,0},{2,3},{3,2},{4,5},{5,4},{6,7},{7,6},{8,9},{9,8},{10,11... | collective-permute-start | bytes 1572872 | tf_op jit(solution)/shard_map/ppermute | solution.py:357
  371.8 12.2 %collective-permute-start.33 = (bf16[128,1024]{1,0:T(8,128)(2,1)}, bf16[128,1024]{1,0:T(8,128)(2,1)S(1)}, u32[]{:S(2)}, u32[]{:S(2)}) collective-permute-start(bf16[128,1024]{1,0:T(8,128)(2,1)} %reduce-scatter.2.cloned.1.call-done), channel_id=1, source_target_pairs={{0,2},{2,0},{1,3},{3,1},{4,6},{6,4},{5,7},{7,5},{8,10},{10,8},{9,1... | collective-permute-start | bytes 786440 | tf_op jit(solution)/shard_map/ppermute | solution.py:524
  384.8 123.2 %collective-permute-start.34 = (f32[128,1024]{1,0:T(8,128)S(1)}, f32[128,1024]{1,0:T(8,128)S(1)}, u32[]{:S(2)}, u32[]{:S(2)}) collective-permute-start(f32[128,1024]{1,0:T(8,128)S(1)} %convert_add_fusion.4), channel_id=1, source_target_pairs={{0,1},{1,0},{2,3},{3,2},{4,5},{5,4},{6,7},{7,6},{8,9},{9,8},{10,11... | collective-permute-start | bytes 1572872 | tf_op jit(solution)/shard_map/ppermute | solution.py:357
  (43 other events, 72.1 us)
Sparse Core Ops, SparseCore 0:
  10.7 60.0 all-gather.2
  301.0 70.7 reduce-scatter.1
  377.7 126.2 all-reduce.4
